TPU v7x, 256 devices: a whole 4x4x8 slice. The times are simulated.
256 devices in a mesh: seq: 64 (over x, z_hi, y, core), tp: 4 (over z_lo).
Axes of the slice: x: 4, y: 4, z: 8 (z_hi: 2, z_lo: 4; z = z_hi * 4 + z_lo), core: 2. Of those that a mesh axis runs over, the one named last changes fastest.
Arguments:
- projected: float32 [3, 32768, 4096], P(None, 'seq', 'tp'), may hold values from -6 to 6
- short_filter: float32 [3, 7, 4096], P(None, None, 'tp'), may hold values from -2 to 2
- long_filter: float32 [4, 32768], P(None, ('seq', 'tp')), may hold values from -0.03125 to 0.03125
- skip_gain: float32 [4096], P('tp'), may hold values from 0.1 to 1.9
Outputs:
- mixed: float32 [32768, 4096], P('seq', 'tp')
All inputs are finite; a program needn't handle non-finite values.
Results may differ from a plain program's by a relative error of at most 0.000098.
Values sent between devices are 32-bit elements; how exact they have to be, the bound alone decides.
No kernel may reach another device: no remote copies, remote signals or barrier semaphores. Data moves between devices by JAX's collectives and lax.ppermute only.
A program may use at most 128 MiB of HBM per device.

v0:
```python
import jax
import jax.numpy as jnp
from jax import lax
from jax.sharding import PartitionSpec as P

two_pi = 6.283185307179586
highest = lax.Precision.HIGHEST


def passed_along(x, axis, by):
    devices = lax.axis_size(axis)
    pairs = [(i, i + by) for i in range(devices) if 0 <= i + by < devices]
    return lax.ppermute(x, axis, pairs)


def turns(height, breadth, modulus):
    row_index = lax.broadcasted_iota(jnp.int32, (height, breadth), 0)
    col_index = lax.broadcasted_iota(jnp.int32, (height, breadth), 1)
    angles = (row_index * col_index % modulus).astype(jnp.float32) * (two_pi / modulus)
    return (jnp.cos(angles), -jnp.sin(angles))


def forward(signal):
    signals = signal.shape[0]
    length = signal.shape[1]
    full_length = 2 * length
    columns = 128
    blocks = full_length // columns
    shaped = signal.reshape(signals, blocks // 2, columns)
    first_re, first_im = turns(blocks, blocks // 2, blocks)
    section_re = jnp.einsum("kn,cnm->ckm", first_re, shaped, precision=highest)
    section_im = jnp.einsum("kn,cnm->ckm", first_im, shaped, precision=highest)
    twist_re, twist_im = turns(blocks, columns, full_length)
    bent_re = section_re * twist_re - section_im * twist_im
    bent_im = section_re * twist_im + section_im * twist_re
    table_re, table_im = turns(columns, columns, columns)
    out_re = jnp.einsum("ckm,mj->ckj", bent_re, table_re, precision=highest) - jnp.einsum(
        "ckm,mj->ckj", bent_im, table_im, precision=highest
    )
    out_im = jnp.einsum("ckm,mj->ckj", bent_re, table_im, precision=highest) + jnp.einsum(
        "ckm,mj->ckj", bent_im, table_re, precision=highest
    )
    return (out_re, out_im)


def inverse(spec_re, spec_im, length):
    signals = spec_re.shape[0]
    full_length = 2 * length
    columns = 128
    blocks = full_length // columns
    table_re, table_im = turns(columns, columns, columns)
    back_re = jnp.einsum("ckj,jm->ckm", spec_re, table_re, precision=highest) + jnp.einsum(
        "ckj,jm->ckm", spec_im, table_im, precision=highest
    )
    back_im = jnp.einsum("ckj,jm->ckm", spec_im, table_re, precision=highest) - jnp.einsum(
        "ckj,jm->ckm", spec_re, table_im, precision=highest
    )
    twist_re, twist_im = turns(blocks, columns, full_length)
    bent_re = back_re * twist_re + back_im * twist_im
    bent_im = back_im * twist_re - back_re * twist_im
    first_re, first_im = turns(blocks // 2, blocks, blocks)
    result = jnp.einsum("nk,ckm->cnm", first_re, bent_re, precision=highest) + jnp.einsum(
        "nk,ckm->cnm", first_im, bent_im, precision=highest
    )
    return result.reshape(signals, length) / full_length


def body(projected, short_filter, long_filter, skip_gain):
    row_count = projected.shape[1]
    width_local = projected.shape[2]
    taps_count = short_filter.shape[1]
    previous = passed_along(projected[:, row_count - (taps_count - 1) :, :], "seq", 1)
    extended = jnp.concatenate([previous, projected], axis=1)
    features = short_filter[:, 0:1, :] * extended[:, 0:row_count, :]
    for offset in range(1, taps_count):
        features = (
            features
            + short_filter[:, offset : offset + 1, :] * extended[:, offset : offset + row_count, :]
        )
    gate_rows = features[0]
    product = features[1] * features[2]
    seq_count = lax.axis_size("seq")
    per_device = width_local // seq_count
    total_width = width_local * lax.axis_size("tp")
    groups = long_filter.shape[0]
    whole_filter = lax.all_gather(long_filter, ("seq", "tp"), axis=1, tiled=True)
    length = whole_filter.shape[1]
    first_channel = lax.axis_index("tp") * width_local + lax.axis_index("seq") * per_device
    group_index = first_channel // (total_width // groups)
    every_re, every_im = forward(whole_filter)
    selector = (lax.broadcasted_iota(jnp.int32, (groups, 1, 1), 0) == group_index).astype(
        jnp.float32
    )
    spec_re = jnp.sum(selector * every_re, axis=0, keepdims=True)
    spec_im = jnp.sum(selector * every_im, axis=0, keepdims=True)
    series = lax.all_to_all(
        product.T.reshape(seq_count, per_device, row_count),
        "seq",
        split_axis=0,
        concat_axis=2,
        tiled=True,
    )[0]
    series_re, series_im = forward(series)
    prod_re = series_re * spec_re - series_im * spec_im
    prod_im = series_re * spec_im + series_im * spec_re
    returned = lax.all_to_all(
        inverse(prod_re, prod_im, length)[None], "seq", split_axis=2, concat_axis=0, tiled=True
    )
    long_out = returned.reshape(width_local, row_count).T
    mixed = gate_rows * (long_out + skip_gain * product)
    return mixed


def solution(mesh):
    placed = (P(None, "seq", "tp"), P(None, None, "tp"), P(None, ("seq", "tp")), P("tp"))
    return jax.shard_map(
        body, mesh=mesh, in_specs=placed, out_specs=P("seq", "tp"), check_vma=False
    )
```

profile of v0, /device:TPU:1, one launch (start us, length us, event | category | flops | bytes accessed | tf_op | source)
XLA Modules:
  0.0 1111.1 jit_solution(11635221424564926077)
XLA Ops:
  0.9 4.6 collective-permute-start
  7.1 6.5 copy.35
  14.1 29.3 %fusion.4 = f32[3,512,1024]{1,2,0:T(8,128)S(1)} fusion(f32[3,512,1024]{1,2,0:T(8,128)} %copy.35, f32[3,6,1024]{1,2,0:T(8,128)S(1)} %copy.34, f32[3,1024]{1,0:T(4,128)S(1)} %get-tuple-element.12, f32[3,1024]{1,0:T(4,128)S(1)} %get-tuple-element.13, f32[3,1024]{1,0:T(4,128)S(1)} %get-tuple-element.14, f32[3,1024]{1,0:T(4,128)S(1)} %get-tuple-element.15, ...), kind=kLoop, calls=%fused_computation.14 | loop fusion | flops 29884416 | bytes 12742656 | tf_op jit(solution)/shard_map/add | solution.py:77
  47.9 14.1 %all-to-all-start = ((f32[64,16,512]{2,1,0:T(8,128)}), f32[64,16,512]{2,1,0:T(8,128)S(1)}, u32[]{:S(2)}, u32[]{:S(2)}) async-start(f32[64,16,512]{2,1,0:T(8,128)} %bitcast.3), calls=%async_computation | async-start | bytes 4194304 | tf_op jit(solution)/shard_map/all_to_all | solution.py:96
  63.3 657.2 %all_gather.3 = f32[4,32768]{1,0:T(4,128)S(1)} all-gather(f32[4,128]{1,0:T(4,128)S(1)} %copy-done.3), channel_id=1, replica_groups=mesh['seq'=64,'tp'=4] {'seq','tp'}, dimensions={1}, use_global_device_ids=true | all-gather | bytes 526336 | tf_op jit(solution)/shard_map/all_gather | solution.py:86
  737.1 8.7 fusion.65
  745.8 9.1 fusion.68
  754.9 7.7 fusion.42
  762.7 7.4 fusion.44
  770.1 7.8 convolution_add_fusion.1
  777.9 7.6 convolution_subtract_fusion.1
  785.5 5.4 fusion.39
  790.9 5.0 fusion.38
  795.9 5.4 convolution_subtract_fusion
  801.3 5.2 convolution_add_fusion
  806.5 6.0 fusion.19
  812.6 6.0 multiply_bitcast_fusion
  818.6 13.6 %copy.65 = f32[16,256,128]{0,2,1:T(8,128)} copy(f32[16,256,128]{1,2,0:T(8,128)S(1)} %multiply_bitcast_fusion) | data formatting | bytes 4194304 | tf_op jit(solution)/shard_map/div | solution.py:65
  832.7 146.5 %reduce = f32[32768,16]{1,0:T(8,128)} reduce(f32[32768,1,16]{2,1,0:T(1,128)} %bitcast.128, f32[]{:T(128)} %broadcast.239), dimensions={1}, to_apply=%bitcast.122.reduce_sub_computation | reduce | bytes 4194308
  979.2 11.8 %reshape.71 = f32[64,1,8192]{2,1,0:T(1,128)S(1)} reshape(f32[32768,16]{1,0:T(8,128)} %reduce) | data formatting | bytes 4194304
  991.0 62.9 %all_to_all.30 = f32[64,1,8192]{2,1,0:T(1,128)} all-to-all(f32[64,1,8192]{2,1,0:T(1,128)S(1)} %reshape.71), channel_id=1, replica_groups=mesh['seq'=64,'tp'=4] {'seq'}, dimensions={0} | all-to-all | bytes 4194304 | tf_op jit(solution)/shard_map/all_to_all | solution.py:106
  1053.9 7.5 reduce.1
  1061.4 33.1 %reshape.72 = f32[32768,1,16]{2,1,0:T(1,128)} reshape(f32[64,8192]{1,0:T(8,128)S(1)} %reduce.1) | data formatting | bytes 4194304
  1094.6 10.0 copy.66
  (34 shorter events, 32.0 us)
Async XLA Ops:
  0.9 12.7 %collective-permute-start = (f32[3,6,1024]{2,1,0:T(8,128)S(1)}, f32[3,6,1024]{2,1,0:T(8,128)S(1)}, u32[]{:S(2)}, u32[]{:S(2)}) collective-permute-start(f32[3,6,1024]{2,1,0:T(8,128)S(1)} %slice.52), channel_id=1, source_target_pairs={{0,4},{4,8},{8,12},{12,16},{16,20},{20,24},{24,28},{28,32},{32,36}... | collective-permute-start | bytes 221192 | tf_op jit(solution)/shard_map/ppermute | solution.py:13
  43.5 2.6 copy-start
  47.8 15.4 %copy-start.3 = (f32[4,128]{1,0:T(4,128)S(1)}, f32[4,128]{1,0:T(4,128)}, u32[]{:S(2)}) copy-start(f32[4,128]{1,0:T(4,128)} %param.6) | copy-start | bytes 6148
  47.9 684.9 %all-to-all-start = ((f32[64,16,512]{2,1,0:T(8,128)}), f32[64,16,512]{2,1,0:T(8,128)S(1)}, u32[]{:S(2)}, u32[]{:S(2)}) async-start(f32[64,16,512]{2,1,0:T(8,128)} %bitcast.3), calls=%async_computation | async-start | bytes 4194304 | tf_op jit(solution)/shard_map/all_to_all | solution.py:96
  63.2 665.8 %copy-start.1 = (f32[512,128]{1,0:T(8,128)}, f32[512,128]{1,0:T(8,128)S(1)}, u32[]{:S(2)}) copy-start(f32[512,128]{1,0:T(8,128)S(1)} %copy.42) | copy-start | bytes 786436
  1104.6 1.2 copy-start.2
where the time goes:
time: 1120 us; the launch traced here: 1110 us
  blocking collectives  720 us (64%)
  other arithmetic  190 us (17%)
  matrix products  93.6 us (8%)
  local copies, waits for them, and re-layouts  88.7 us (8%)
  starting transfers between devices  18.7 us (2%)
    all_gather x1, blocking collectives, body(): lax.all_gather(long_filter, ('seq', 'tp'), axis=1, tiled=True)  657 us
    unnamed x1, other arithmetic  147 us
    all_to_all x1, blocking collectives, body(): lax.all_to_all(inverse(prod_re, prod_im, length)[None], 'seq', split_axis...  62.9 us
    unnamed x16, local copies, waits for them, and re-layouts  54.6 us
    add x1, other arithmetic, body(): features + short_filter[:, offset:offset + 1, :] * extended[:, offset:off...  29.3 us
  transfers between devices with their start and end apart: 2, of which 0 were waited for; matrix products, arithmetic and copies ran while one was open for 2% of the time, Pallas kernels for 0%

commit v1 on v0

v1 whole, which is shorter than its diff:
```python
import functools

import jax
import jax.numpy as jnp
import ml_dtypes
import numpy as np
from jax import lax
from jax.experimental import pallas as pl
from jax.experimental.pallas import tpu as pltpu
from jax.sharding import Mesh
from jax.sharding import PartitionSpec as P

f32 = jnp.float32
bf16 = jnp.bfloat16

ROWS = 512
TAPS = 7
LANES = 128
PEERS = 32
PIECE = 8
QUARTERS = ROWS // LANES
BLOCK = QUARTERS * PIECE
HALF = PEERS * BLOCK
LENGTH = 32768
VMEM_BYTES = 60 << 20
ORDER = 256

SEQ = ("x", "zh", "y", "core")
PLANE = ("x", "y", "core")


def split_np(table):
    high = table.astype(np.float32).astype(ml_dtypes.bfloat16)
    low = (table - high.astype(np.float64)).astype(ml_dtypes.bfloat16)
    return high, low


def position_blocks():
    n1 = np.zeros((2, 4, PEERS), np.int64)
    for z in range(2):
        for q in range(4):
            for p in range(PEERS):
                x, rest = divmod(p, 8)
                n1[z, q, p] = 4 * (x * 16 + z * 8 + rest) + q
    return n1.reshape(-1)


def make_tables():
    n1 = position_blocks()
    k1 = np.arange(ORDER)
    m = np.arange(LANES)
    turn = 2.0 * np.pi
    first = turn * (((4 * k1[:, None] + 1) * n1[None, :]) % (4 * ORDER)) / (4 * ORDER)
    first = np.concatenate([np.cos(first), -np.sin(first)], axis=0)
    bend = turn * ((4 * k1[:, None] + 1) * m[None, :]) / (4 * LENGTH)
    second = turn * ((m[:, None] * m[None, :]) % LANES) / LANES
    cosine, sine = np.cos(second), np.sin(second)
    onward = np.block([[cosine, -sine], [sine, cosine]])
    back = np.block([[cosine, sine], [-sine, cosine]])
    last = first.T
    first_high, first_low = split_np(first)
    onward_high, onward_low = split_np(onward)
    back_high, back_low = split_np(back)
    last_high, last_low = split_np(last)
    return dict(
        first=np.concatenate([first_high, first_high, first_low], axis=1),
        last=np.concatenate([last_high, last_high, last_low], axis=1),
        onward=np.concatenate([onward_high, onward_high, onward_low], axis=0),
        back=np.concatenate([back_high, back_high, back_low], axis=0),
        bend=np.stack([np.cos(bend), -np.sin(bend)]).astype(np.float32),
    )


def halves(x):
    high = x.astype(bf16)
    low = (x - high.astype(f32)).astype(bf16)
    return high, low


def dot(a, b):
    return jnp.dot(a, b, preferred_element_type=f32)


def to_spectrum(columns, first, onward, bend):
    high, low = halves(columns)
    section = dot(first, jnp.concatenate([high, low, high], axis=0))
    bend_re, bend_im = bend[0], bend[1]
    rows = []
    for at in range(columns.shape[1] // LANES):
        re = section[:ORDER, at * LANES : (at + 1) * LANES]
        im = section[ORDER:, at * LANES : (at + 1) * LANES]
        rows.append(
            jnp.concatenate([re * bend_re - im * bend_im, re * bend_im + im * bend_re], axis=1)
        )
    bent = jnp.concatenate(rows, axis=0)
    high, low = halves(bent)
    return dot(jnp.concatenate([high, low, high], axis=1), onward)


def from_spectrum(spectrum, last, back, bend):
    high, low = halves(spectrum)
    section = dot(jnp.concatenate([high, low, high], axis=1), back)
    bend_re, bend_im = bend[0], bend[1]
    columns = []
    for at in range(spectrum.shape[0] // ORDER):
        re = section[at * ORDER : (at + 1) * ORDER, :LANES]
        im = section[at * ORDER : (at + 1) * ORDER, LANES:]
        columns.append(
            jnp.concatenate([re * bend_re + im * bend_im, im * bend_re - re * bend_im], axis=0)
        )
    bent = jnp.concatenate(columns, axis=1)
    high, low = halves(bent)
    return dot(last, jnp.concatenate([high, low, high], axis=0))


def conv_kernel(
    layout,
    sources,
    z_ref,
    *refs,
):
    own_ref, other_ref, spectrum_ref = (refs[:sources] * 3)[:3]
    first_ref, last_ref, onward_ref, back_ref, bend_ref = refs[sources : sources + 5]
    out_refs = refs[sources + 5 :]
    own_at, own_stride, other_at, other_stride, taps_at = layout
    low_plane = z_ref[0] == 0
    bend = bend_ref[...]
    if taps_at is not None:
        pieces = [spectrum_ref[pl.ds(taps_at + zq, PEERS, stride=own_stride), :] for zq in range(8)]
        taps = to_spectrum(jnp.concatenate(pieces, axis=0), first_ref[...], onward_ref[...], bend)
        taps = taps * (1.0 / LENGTH)
        out_refs[2][...] = taps
    else:
        taps = spectrum_ref[...]
    taps_re = taps[:, :LANES]
    taps_im = taps[:, LANES:]
    for pair in range(PIECE // 2):
        columns = []
        for channel in (2 * pair, 2 * pair + 1):
            own, other = [], []
            for q in range(4):
                row = q * PIECE + channel
                own.append(own_ref[pl.ds(own_at + row, PEERS, stride=own_stride), :])
                other.append(other_ref[pl.ds(other_at + row, PEERS, stride=other_stride), :])
            own = jnp.concatenate(own, axis=0)
            other = jnp.concatenate(other, axis=0)
            columns.append(
                jnp.concatenate(
                    [jnp.where(low_plane, own, other), jnp.where(low_plane, other, own)], axis=0
                )
            )
        spectrum = to_spectrum(
            jnp.concatenate(columns, axis=1), first_ref[...], onward_ref[...], bend
        )
        rows = []
        for at in range(2):
            re = spectrum[at * ORDER : (at + 1) * ORDER, :LANES]
            im = spectrum[at * ORDER : (at + 1) * ORDER, LANES:]
            rows.append(
                jnp.concatenate([re * taps_re - im * taps_im, re * taps_im + im * taps_re], axis=1)
            )
        result = from_spectrum(
            jnp.concatenate(rows, axis=0), last_ref[...], back_ref[...], bend
        )
        for at, channel in enumerate((2 * pair, 2 * pair + 1)):
            upper = result[: ORDER // 2, at * LANES : (at + 1) * LANES]
            lower = result[ORDER // 2 :, at * LANES : (at + 1) * LANES]
            own = jnp.where(low_plane, upper, lower)
            other = jnp.where(low_plane, lower, upper)
            for q in range(4):
                row = q * PIECE + channel
                rows_own = own[q * PEERS : (q + 1) * PEERS]
                rows_other = other[q * PEERS : (q + 1) * PEERS]
                if len(out_refs) == 1:
                    out_refs[0][pl.ds(row, PEERS, stride=2 * BLOCK), :] = rows_own
                    out_refs[0][pl.ds(BLOCK + row, PEERS, stride=2 * BLOCK), :] = rows_other
                else:
                    out_refs[0][pl.ds(row, PEERS, stride=BLOCK), :] = rows_own
                    out_refs[1][pl.ds(row, PEERS, stride=BLOCK), :] = rows_other


def feature_kernel(
    z_ref, proj_ref, halo_ref, short_ref, skip_ref, sent_ref, gate_ref, direct_ref, long_ref
):
    step = 64
    for j in range(3):
        long_ref[j, 0:8, :] = halo_ref[j]
        long_ref[j, 8 : ROWS + 8, :] = proj_ref[j]
    skip = skip_ref[0:1, :]
    for start in range(0, ROWS, LANES):
        parts = []
        for at in range(start, start + LANES, step):
            features = []
            for j in range(3):
                total = short_ref[j, 0:1, :] * long_ref[j, at + 2 : at + 2 + step, :]
                for i in range(1, TAPS):
                    total = total + short_ref[j, i : i + 1, :] * long_ref[
                        j, at + 2 + i : at + 2 + i + step, :
                    ]
                features.append(total)
            product = features[1] * features[2]
            gate_ref[at : at + step, :] = features[0]
            direct_ref[at : at + step, :] = features[0] * (skip * product)
            parts.append(product)
        turned = jnp.concatenate(parts, axis=0).T
        sent_ref[:, start // LANES] = turned.reshape(LANES // PIECE, PIECE, LANES)


def final_kernel(z_ref, long_ref, gate_ref, direct_ref, *rest):
    out_ref = rest[-1]
    for start in range(0, ROWS, LANES):
        turned = long_ref[:, start // LANES].reshape(LANES, LANES).T
        out_ref[start : start + LANES, :] = (
            gate_ref[start : start + LANES, :] * turned + direct_ref[start : start + LANES, :]
        )


def block_of(z, slot, half, chunk):
    plane = z if slot == 0 else 1 - z
    return chunk * 4 + plane * 2 + half


def features_of(z, chunk, slots, projected, halo, short_filter, skip):
    count = len(slots)

    def column(i, z_ref):
        plane = z_ref[0]
        if slots == (1,):
            plane = 1 - plane
        elif count == 2:
            plane = jnp.where(i // 2 == 0, plane, 1 - plane)
        return chunk * 4 + plane * 2 + i % 2

    blocks = 2 * count
    return pl.pallas_call(
        feature_kernel,
        grid_spec=pltpu.PrefetchScalarGridSpec(
            num_scalar_prefetch=1,
            grid=(blocks,),
            in_specs=[
                pl.BlockSpec((3, ROWS, LANES), lambda i, z: (0, 0, column(i, z))),
                pl.BlockSpec((3, 8, LANES), lambda i, z: (0, 0, column(i, z))),
                pl.BlockSpec((3, TAPS, LANES), lambda i, z: (0, 0, column(i, z))),
                pl.BlockSpec((1, LANES), lambda i, z: (0, column(i, z))),
            ],
            out_specs=[
                pl.BlockSpec(
                    (LANES // PIECE, None, QUARTERS, PIECE, LANES),
                    lambda i, z: (i % 2, i // 2, 0, 0, 0),
                ),
                pl.BlockSpec((ROWS, LANES), lambda i, z: (0, i)),
                pl.BlockSpec((ROWS, LANES), lambda i, z: (0, i)),
            ],
            scratch_shapes=[pltpu.VMEM((3, ROWS + 8, LANES), f32)],
        ),
        out_shape=[
            jax.ShapeDtypeStruct((PEERS, count, QUARTERS, PIECE, LANES), f32),
            jax.ShapeDtypeStruct((ROWS, blocks * LANES), f32),
            jax.ShapeDtypeStruct((ROWS, blocks * LANES), f32),
        ],
        compiler_params=pltpu.CompilerParams(vmem_limit_bytes=VMEM_BYTES),
        cost_estimate=pl.CostEstimate(
            flops=blocks * 6_000_000, bytes_accessed=blocks * 1_600_000, transcendentals=0
        ),
        name="features",
    )(z, projected, halo, short_filter, skip)


def finish(z, chunk, slots, long_out, in_slot, gate, direct, gate_at, whole):
    count = len(slots)

    def column(i, z_ref):
        plane = z_ref[0]
        if slots == (1,):
            plane = 1 - plane
        elif count == 2:
            plane = jnp.where(i // 2 == 0, plane, 1 - plane)
        return chunk * 4 + plane * 2 + i % 2

    operands = [z, long_out, gate, direct]
    in_specs = [
        pl.BlockSpec(
            (LANES // PIECE, None, QUARTERS, PIECE, LANES),
            lambda i, z: (i % 2, in_slot + i // 2, 0, 0, 0),
        ),
        pl.BlockSpec((ROWS, LANES), lambda i, z: (0, gate_at + i)),
        pl.BlockSpec((ROWS, LANES), lambda i, z: (0, gate_at + i)),
    ]
    aliases = {}
    if whole is not None:
        aliases = {len(operands): 0}
        operands.append(whole)
        in_specs.append(pl.BlockSpec(memory_space=pl.ANY))
    return pl.pallas_call(
        final_kernel,
        grid_spec=pltpu.PrefetchScalarGridSpec(
            num_scalar_prefetch=1,
            grid=(2 * count,),
            in_specs=in_specs,
            out_specs=pl.BlockSpec((ROWS, LANES), lambda i, z: (0, column(i, z))),
        ),
        out_shape=jax.ShapeDtypeStruct((ROWS, 8 * LANES), f32),
        input_output_aliases=aliases,
        compiler_params=pltpu.CompilerParams(vmem_limit_bytes=VMEM_BYTES),
        cost_estimate=pl.CostEstimate(
            flops=count * 300_000, bytes_accessed=count * 2_100_000, transcendentals=0
        ),
        name="finish",
    )(*operands)


def convolve(z, layout, sources, tables, joined):
    if joined:
        out_shape = [jax.ShapeDtypeStruct((2 * HALF, LANES), f32)]
    else:
        out_shape = [jax.ShapeDtypeStruct((HALF, LANES), f32)] * 2
        out_shape = out_shape + [jax.ShapeDtypeStruct((ORDER, 2 * LANES), f32)]
    operands = list(sources) + [
        tables[name] for name in ("first", "last", "onward", "back", "bend")
    ]
    return pl.pallas_call(
        functools.partial(conv_kernel, layout, len(sources)),
        grid_spec=pltpu.PrefetchScalarGridSpec(
            num_scalar_prefetch=1,
            grid=(1,),
            in_specs=[whole_spec(x.shape) for x in operands],
            out_specs=[whole_spec(x.shape) for x in out_shape],
        ),
        out_shape=out_shape,
        compiler_params=pltpu.CompilerParams(vmem_limit_bytes=VMEM_BYTES),
        cost_estimate=pl.CostEstimate(
            flops=3_300_000_000, bytes_accessed=5_000_000, transcendentals=0
        ),
        name="convolve",
    )(z, *operands)


def whole_spec(shape):
    return pl.BlockSpec(shape, lambda i, z: (0,) * len(shape))


def swap_planes(x):
    return lax.ppermute(x, "zh", [(0, 1), (1, 0)])


def across(x):
    return lax.all_to_all(x, PLANE, split_axis=0, concat_axis=0, tiled=True)


def body(projected, short_filter, long_filter, skip_gain):
    tables = {name: jnp.asarray(table) for name, table in make_tables().items()}
    z = lax.axis_index("zh").astype(jnp.int32).reshape(1)
    skip = skip_gain.reshape(1, -1)
    devices = lax.axis_size(SEQ)
    halo = lax.ppermute(
        projected[:, ROWS - 8 :, :], SEQ, [(i, i + 1) for i in range(devices - 1)]
    )
    feature = functools.partial(
        features_of, projected=projected, halo=halo, short_filter=short_filter, skip=skip
    )
    a_other, gate_ao, direct_ao = feature(z, 0, (1,))
    a_from = swap_planes(a_other)
    z1, _ = lax.optimization_barrier((z, a_other))
    b_both, gate_b, direct_b = feature(z1, 1, (0, 1))
    b_here = across(b_both)
    z2, _ = lax.optimization_barrier((z, a_other))
    a_own, gate_a, direct_a = feature(z2, 0, (0,))

    pieces, _ = lax.optimization_barrier((long_filter, a_other))
    pieces = jnp.concatenate([pieces, pieces], axis=0)
    taps = lax.all_to_all(pieces, ("zh", "zl"), split_axis=0, concat_axis=0, tiled=True)

    a_from, b_here, taps = lax.optimization_barrier((a_from, b_here, taps))
    b_from = swap_planes(b_here[:, 1])
    a_here = across(
        jnp.concatenate(
            [
                a_own.reshape(PEERS, BLOCK, LANES),
                a_from.reshape(PEERS, BLOCK, LANES),
                jnp.broadcast_to(taps[None], (PEERS, 8, LANES)),
            ],
            axis=1,
        )
    )
    a_flat = a_here.reshape(-1, LANES)
    wide = 2 * BLOCK + 8
    conv_a_own, conv_a_other, spectrum = convolve(
        z, (0, wide, BLOCK, wide, 2 * BLOCK), (a_flat,), tables, False
    )
    a_back = swap_planes(conv_a_other)
    z3, _ = lax.optimization_barrier((z, conv_a_other))
    (conv_b,) = convolve(
        z3,
        (0, 2 * BLOCK, 0, BLOCK, None),
        (b_here.reshape(2 * HALF, LANES), b_from.reshape(HALF, LANES), spectrum),
        tables,
        True,
    )
    b_out = across(conv_b.reshape(PEERS, 2, QUARTERS, PIECE, LANES))
    a_back, b_out = lax.optimization_barrier((a_back, b_out))
    b_back = swap_planes(b_out[:, 1])
    a_out = across(
        jnp.stack([conv_a_own, a_back], 0)
        .reshape(2, PEERS, QUARTERS, PIECE, LANES)
        .transpose(1, 0, 2, 3, 4)
    )
    mixed = finish(z, 1, (0,), b_out, 0, gate_b, direct_b, 0, None)
    mixed = finish(z, 0, (0,), a_out, 0, gate_a, direct_a, 0, mixed)
    mixed = finish(z, 0, (1,), a_out, 1, gate_ao, direct_ao, 0, mixed)
    mixed = finish(z, 1, (1,), b_back[:, None], 0, gate_b, direct_b, 2, mixed)
    return mixed


def solution(mesh):
    fine = Mesh(mesh.devices.reshape(4, 2, 4, 2, 4), ("x", "zh", "y", "core", "zl"))
    placed = (P(None, SEQ, "zl"), P(None, None, "zl"), P(None, SEQ + ("zl",)), P("zl"))
    return jax.shard_map(
        body, mesh=fine, in_specs=placed, out_specs=P(SEQ, "zl"), check_vma=False
    )
```

time: 1120 us -> 183 us (0.16)
  blocking collectives: 720 us -> 0 us
  other arithmetic: 190 us -> 4.27 us
  matrix products: 93.6 us -> 0 us
  local copies, waits for them, and re-layouts: 88.7 us -> 5.26 us
  waiting for transfers between devices: 0.01 us -> 72.6 us
  Pallas kernels: 0 us -> 40.5 us
  starting transfers between devices: 18.7 us -> 59 us
    all_gather x1 -> x0, blocking collectives: 657 us -> none  [body(): lax.all_gather(long_filter, ('seq', 'tp'), axis=1, tiled=True)]
    unnamed x1 -> x0, other arithmetic: 147 us -> none
    dot_general x18 -> x0, matrix products: 93.6 us -> none  [the longest x2 12.1 us: forward(): section_re = jnp.einsum('kn,cnm->ckm', first_re, shaped, precision=highest)]
    all_to_all x1 -> x0, blocking collectives: 62.9 us -> none  [body(): lax.all_to_all(inverse(prod_re, prod_im, length)[None], 'seq', split_axis...]
    unnamed x16 -> x22, local copies, waits for them, and re-layouts: 54.6 us -> 4.28 us
    ppermute x1 -> x5, waiting for transfers between devices: 0.01 us -> 43.9 us  [the longest x4 42.3 us: swap_planes(): return lax.ppermute(x, 'zh', [(0, 1), (1, 0)])]
    pallas_call x0 -> x9, Pallas kernels: none -> 40.5 us  [the longest x2 20.5 us: convolve(): pl.pallas_call(functools.partial(conv_kernel, layout, len(sources)), grid...]
    add x1 -> x0, other arithmetic: 29.3 us -> none  [body(): features + short_filter[:, offset:offset + 1, :] * extended[:, offset:off...]
  transfers between devices with their start and end apart: 2 -> 10, of which waited for: 0 -> 6; matrix products, arithmetic and copies ran while one was open for 2% -> 0% of each run, Pallas kernels for 0% -> 14%
where the time goes in v1:
time: 183 us; the launch traced here: 182 us
  waiting for transfers between devices  72.6 us (40%)
  starting transfers between devices  59 us (32%)
  Pallas kernels  40.5 us (22%)
  local copies, waits for them, and re-layouts  5.26 us (3%)
  other arithmetic  4.27 us (2%)
    ppermute x4, waiting for transfers between devices, swap_planes(): return lax.ppermute(x, 'zh', [(0, 1), (1, 0)])  42.3 us
    all_to_all x4, starting transfers between devices, across(): return lax.all_to_all(x, PLANE, split_axis=0, concat_axis=0, tiled=True)  33.9 us
    all_to_all x4, waiting for transfers between devices, across(): return lax.all_to_all(x, PLANE, split_axis=0, concat_axis=0, tiled=True)  27.3 us
    pallas_call x2, Pallas kernels, convolve(): pl.pallas_call(functools.partial(conv_kernel, layout, len(sources)), grid...  20.5 us
    ppermute x4, starting transfers between devices, swap_planes(): return lax.ppermute(x, 'zh', [(0, 1), (1, 0)])  12.3 us
    pallas_call x3, Pallas kernels, features_of(): pl.pallas_call(feature_kernel, grid_spec=pltpu.PrefetchScalarGridSpec(num...  11.2 us
    pallas_call x4, Pallas kernels, finish(): pl.pallas_call(final_kernel, grid_spec=pltpu.PrefetchScalarGridSpec(num_s...  8.77 us
    all_to_all x1, starting transfers between devices, body(): lax.all_to_all(pieces, ('zh', 'zl'), split_axis=0, concat_axis=0, tiled=T...  8.19 us
  transfers between devices with their start and end apart: 10, of which 6 were waited for; matrix products, arithmetic and copies ran while one was open for 0% of the time, Pallas kernels for 14%

profile of v1, /device:TPU:1, one launch (start us, length us, event | category | flops | bytes accessed | tf_op | source)
XLA Modules:
  0.0 181.7 jit_solution(2878407496261618027)
XLA Ops:
  0.9 4.6 %collective-permute-start = (f32[3,8,1024]{2,1,0:T(8,128)S(1)}, f32[3,8,1024]{2,1,0:T(8,128)S(1)}, u32[]{:S(2)}, u32[]{:S(2)}) collective-permute-start(f32[3,8,1024]{2,1,0:T(8,128)S(1)} %slice.9), channel_id=1, source_target_pairs={{0,4},{4,8},{8,12},{12,16},{16,20},{20,24},{24,28},{28,32},{32,36}... | collective-permute-start | bytes 294920 | tf_op jit(solution)/shard_map/ppermute | solution.py:355
  7.7 3.0 %features.3 = (f32[32,1,4,8,128]{4,3,2,1,0:T(8,128)}, f32[512,256]{1,0:T(8,128)}, f32[512,256]{1,0:T(8,128)}) custom-call(s32[1]{0:T(128)} %bitcast.z_ref, f32[3,512,1024]{2,1,0:T(8,128)} %proj_ref.5, f32[3,8,1024]{2,1,0:T(8,128)} %copy-done.4, f32[3,7,1024]{2,1,0:T(8,128)} %short_ref.5, f32[1,1024]{1,0:T(1,128)} %bitcast.27), custom_call_target="tpu_custom_call" | custom-call | flops 12000000 | bytes 3200000 | tf_op jit(solution)/shard_map/features/pallas_call | solution.py:235
  11.4 8.2 %all-to-all-start.1 = ((f32[8,1,128]{2,1,0:T(1,128)}), f32[8,1,128]{2,1,0:T(1,128)S(1)}, u32[]{:S(2)}, u32[]{:S(2)}) async-start(f32[8,1,128]{2,1,0:T(1,128)} %bitcast.3), calls=%async_computation.1 | async-start | bytes 8192 | tf_op jit(solution)/shard_map/all_to_all | solution.py:371
  19.6 5.2 %features.5 = (f32[32,2,4,8,128]{4,3,2,1,0:T(8,128)}, f32[512,512]{1,0:T(8,128)}, f32[512,512]{1,0:T(8,128)}) custom-call(s32[1]{0:T(128)} %bitcast.z_ref, f32[3,512,1024]{2,1,0:T(8,128)} %proj_ref.5, f32[3,8,1024]{2,1,0:T(8,128)} %copy-done.4, f32[3,7,1024]{2,1,0:T(8,128)} %short_ref.5, f32[1,1024]{1,0:T(1,128)} %bitcast.28), custom_call_target="tpu_custom_call" | custom-call | flops 24000000 | bytes 6400000 | tf_op jit(solution)/shard_map/features/pallas_call | solution.py:235
  26.1 14.2 %all-to-all-start = ((f32[32,2,4,8,128]{4,3,2,1,0:T(8,128)}), f32[32,2,4,8,128]{4,3,2,1,0:T(8,128)S(1)}, u32[]{:S(2)}, u32[]{:S(2)}) async-start(f32[32,2,4,8,128]{4,3,2,1,0:T(8,128)} %get-tuple-element.28), calls=%async_computation | async-start | bytes 2097152 | tf_op jit(solution)/shard_map/all_to_all | solution.py:347
  40.3 3.4 %collective-permute-start.1 = (f32[32,1,4,8,128]{4,3,2,1,0:T(8,128)S(1)}, f32[32,1,4,8,128]{4,3,2,1,0:T(8,128)S(1)}, u32[]{:S(2)}, u32[]{:S(2)}) collective-permute-start(f32[32,1,4,8,128]{4,3,2,1,0:T(8,128)S(1)} %copy-done.8), channel_id=1, source_target_pairs={{0,32},{32,0},{1,33},{33,1},{2,34},{34,2},{3,35},{35,3},{4,36},{36... | collective-permute-start | bytes 1572872 | tf_op jit(solution)/shard_map/ppermute | solution.py:343
  43.6 3.0 %features.4 = (f32[32,1,4,8,128]{4,3,2,1,0:T(8,128)}, f32[512,256]{1,0:T(8,128)}, f32[512,256]{1,0:T(8,128)}) custom-call(s32[1]{0:T(128)} %bitcast.z_ref, f32[3,512,1024]{2,1,0:T(8,128)} %proj_ref.5, f32[3,8,1024]{2,1,0:T(8,128)} %copy-done.4, f32[3,7,1024]{2,1,0:T(8,128)} %short_ref.5, f32[1,1024]{1,0:T(1,128)} %bitcast.29), custom_call_target="tpu_custom_call" | custom-call | flops 12000000 | bytes 3200000 | tf_op jit(solution)/shard_map/features/pallas_call | solution.py:235
  46.7 22.2 %collective-permute-done.1 = f32[32,1,4,8,128]{4,3,2,1,0:T(8,128)S(1)} collective-permute-done((f32[32,1,4,8,128]{4,3,2,1,0:T(8,128)S(1)}, f32[32,1,4,8,128]{4,3,2,1,0:T(8,128)S(1)}, u32[]{:S(2)}, u32[]{:S(2)}) %collective-permute-start.1) | collective-permute-done | bytes 524320 | tf_op jit(solution)/shard_map/ppermute | solution.py:343
  68.9 2.5 %pad_maximum_fusion = f32[32,72,128]{2,1,0:T(8,128)} fusion(f32[32,8,128]{2,1,0:T(8,128)S(1)} %broadcast_in_dim.4, f32[32,32,128]{2,1,0:T(8,128)S(1)} %bitcast.23, f32[32,32,128]{2,1,0:T(8,128)} %bitcast.24), kind=kLoop, calls=%fused_computation | loop fusion | flops 589824 | bytes 2359296 | tf_op jit(solution)/shard_map/concatenate | solution.py:376
  71.4 8.1 %all-to-all-start.2 = ((f32[32,72,128]{2,1,0:T(8,128)}), f32[32,72,128]{2,1,0:T(8,128)S(1)}, u32[]{:S(2)}, u32[]{:S(2)}) async-start(f32[32,72,128]{2,1,0:T(8,128)} %pad_maximum_fusion), calls=%async_computation.2 | async-start | bytes 2359296 | tf_op jit(solution)/shard_map/all_to_all | solution.py:347
  79.6 3.5 %collective-permute-start.3 = (f32[32,4,8,128]{3,2,1,0:T(8,128)S(1)}, f32[32,4,8,128]{3,2,1,0:T(8,128)S(1)}, u32[]{:S(2)}, u32[]{:S(2)}) collective-permute-start(f32[32,4,8,128]{3,2,1,0:T(8,128)S(1)} %slice_bitcast_fusion.1), channel_id=1, source_target_pairs={{0,32},{32,0},{1,33},{33,1},{2,34},{34,2},{3,35},{35,3},{4,36},{36... | collective-permute-start | bytes 1572872 | tf_op jit(solution)/shard_map/ppermute | solution.py:343
  83.1 14.8 %all-to-all-done.2 = f32[32,72,128]{2,1,0:T(8,128)S(1)} async-done(((f32[32,72,128]{2,1,0:T(8,128)}), f32[32,72,128]{2,1,0:T(8,128)S(1)}, u32[]{:S(2)}, u32[]{:S(2)}) %all-to-all-start.2) | async-done | bytes 1179680 | tf_op jit(solution)/shard_map/all_to_all | solution.py:347
  98.9 10.4 %convolve.2 = (f32[1024,128]{1,0:T(8,128)}, f32[1024,128]{1,0:T(8,128)}, f32[256,256]{1,0:T(8,128)}) custom-call(s32[1]{0:T(128)} %bitcast.z_ref, f32[2304,128]{1,0:T(8,128)} %bitcast.20, bf16[512,768]{1,0:T(8,128)(2,1)} %constant.16.clone.refs_1_.refs_3_, bf16[256,1536]{1,0:T(8,128)(2,1)} %constant.17.clone.refs_2_.refs_4_, ...), custom_call_target="tpu_custom_call" | custom-call | flops 3300000000 | bytes 5000000 | tf_op jit(solution)/shard_map/convolve/pallas_call | solution.py:321
  110.1 10.1 %convolve.3 = f32[2048,128]{1,0:T(8,128)} custom-call(s32[1]{0:T(128)} %bitcast.z_ref, f32[2048,128]{1,0:T(8,128)} %bitcast.19, f32[1024,128]{1,0:T(8,128)} %bitcast.31, f32[256,256]{1,0:T(8,128)} %get-tuple-element.35.refs_2_, bf16[512,768]{1,0:T(8,128)(2,1)} %constant.16.clone.refs_1_.refs_3_, bf16[256,1536]{1,0:T(8,128)(2,1)} %constant.17.clone.refs_2_.refs_4_, ...), custom_call_target="tpu_custom_call" | custom-call | flops 3300000000 | bytes 5000000 | tf_op jit(solution)/shard_map/convolve/pallas_call | solution.py:321
  120.2 4.0 %all-to-all-start.3 = ((f32[32,2,4,8,128]{4,3,2,1,0:T(8,128)}), f32[32,2,4,8,128]{4,3,2,1,0:T(8,128)S(1)}, u32[]{:S(2)}, u32[]{:S(2)}) async-start(f32[32,2,4,8,128]{4,3,2,1,0:T(8,128)} %bitcast.21), calls=%async_computation.3 | async-start | bytes 2097152 | tf_op jit(solution)/shard_map/all_to_all | solution.py:347
  124.3 3.3 %collective-permute-start.2 = (f32[1024,128]{1,0:T(8,128)S(1)}, f32[1024,128]{1,0:T(8,128)S(1)}, u32[]{:S(2)}, u32[]{:S(2)}) collective-permute-start(f32[1024,128]{1,0:T(8,128)S(1)} %copy-done.9), channel_id=1, source_target_pairs={{0,32},{32,0},{1,33},{33,1},{2,34},{34,2},{3,35},{35,3},{4,36},{36... | collective-permute-start | bytes 1572872 | tf_op jit(solution)/shard_map/ppermute | solution.py:343
  127.6 20.1 %collective-permute-done.2 = f32[1024,128]{1,0:T(8,128)S(1)} collective-permute-done((f32[1024,128]{1,0:T(8,128)S(1)}, f32[1024,128]{1,0:T(8,128)S(1)}, u32[]{:S(2)}, u32[]{:S(2)}) %collective-permute-start.2) | collective-permute-done | bytes 524320 | tf_op jit(solution)/shard_map/ppermute | solution.py:343
  148.9 7.5 %all-to-all-start.4 = ((f32[32,2,4,8,128]{4,3,2,1,0:T(8,128)}), f32[32,2,4,8,128]{4,3,2,1,0:T(8,128)S(1)}, u32[]{:S(2)}, u32[]{:S(2)}) async-start(f32[32,2,4,8,128]{4,3,2,1,0:T(8,128)} %maximum_bitcast_fusion), calls=%async_computation.4 | async-start | bytes 2097152 | tf_op jit(solution)/shard_map/all_to_all | solution.py:347
  156.5 2.1 %collective-permute-start.4 = (f32[32,4,8,128]{3,2,1,0:T(8,128)S(1)}, f32[32,4,8,128]{3,2,1,0:T(8,128)S(1)}, u32[]{:S(2)}, u32[]{:S(2)}) collective-permute-start(f32[32,4,8,128]{3,2,1,0:T(8,128)S(1)} %slice_bitcast_fusion), channel_id=1, source_target_pairs={{0,32},{32,0},{1,33},{33,1},{2,34},{34,2},{3,35},{35,3},{4,36},{36... | collective-permute-start | bytes 1572872 | tf_op jit(solution)/shard_map/ppermute | solution.py:343
  158.6 2.2 %finish.4.rest_0_ = f32[512,1024]{1,0:T(8,128)} custom-call(s32[1]{0:T(128)} %bitcast.z_ref, f32[32,2,4,8,128]{4,3,2,1,0:T(8,128)} %copy-done.1, f32[512,512]{1,0:T(8,128)} %get-tuple-element.37.gate_ref, f32[512,512]{1,0:T(8,128)} %get-tuple-element.38.direct_ref), custom_call_target="tpu_custom_call" | custom-call | flops 300000 | bytes 2100000 | tf_op jit(solution)/shard_map/finish/pallas_call | solution.py:294
  160.8 12.5 %all-to-all-done.4.long_ref = f32[32,2,4,8,128]{4,3,2,1,0:T(8,128)S(1)} async-done(((f32[32,2,4,8,128]{4,3,2,1,0:T(8,128)}), f32[32,2,4,8,128]{4,3,2,1,0:T(8,128)S(1)}, u32[]{:S(2)}, u32[]{:S(2)}) %all-to-all-start.4) | async-done | bytes 1048608 | tf_op jit(solution)/shard_map/all_to_all | solution.py:347
  174.3 2.2 %finish.5.rest_0_ = f32[512,1024]{1,0:T(8,128)} custom-call(s32[1]{0:T(128)} %bitcast.z_ref, f32[32,2,4,8,128]{4,3,2,1,0:T(8,128)} %copy-done, f32[512,256]{1,0:T(8,128)} %get-tuple-element.43.gate_ref, f32[512,256]{1,0:T(8,128)} %get-tuple-element.44.direct_ref, f32[512,1024]{1,0:T(8,128)} %finish.4.rest_0_), custom_call_target="tpu_custom_call", output_to_operand_aliasing={{}: (4, {})} | custom-call | flops 300000 | bytes 2100000 | tf_op jit(solution)/shard_map/finish/pallas_call | solution.py:294
  176.5 2.2 %finish.6.rest_0_ = f32[512,1024]{1,0:T(8,128)} custom-call(s32[1]{0:T(128)} %bitcast.z_ref, f32[32,2,4,8,128]{4,3,2,1,0:T(8,128)} %copy-done, f32[512,256]{1,0:T(8,128)} %get-tuple-element.41.gate_ref, f32[512,256]{1,0:T(8,128)} %get-tuple-element.42.direct_ref, f32[512,1024]{1,0:T(8,128)} %finish.5.rest_0_), custom_call_target="tpu_custom_call", output_to_operand_aliasing={{}: (4, {})} | custom-call | flops 300000 | bytes 2100000 | tf_op jit(solution)/shard_map/finish/pallas_call | solution.py:294
  179.5 2.2 %finish.7 = f32[512,1024]{1,0:T(8,128)} custom-call(s32[1]{0:T(128)} %bitcast.z_ref, f32[32,1,4,8,128]{4,3,2,1,0:T(8,128)} %bitcast.26, f32[512,512]{1,0:T(8,128)} %get-tuple-element.37.gate_ref, f32[512,512]{1,0:T(8,128)} %get-tuple-element.38.direct_ref, f32[512,1024]{1,0:T(8,128)} %finish.6.rest_0_), custom_call_target="tpu_custom_call", output_to_operand_aliasing={{}: (4, {})} | custom-call | flops 300000 | bytes 2100000 | tf_op jit(solution)/shard_map/finish/pallas_call | solution.py:294
  (34 shorter events, 10.0 us)
Async XLA Ops:
  0.9 6.2 %collective-permute-start = (f32[3,8,1024]{2,1,0:T(8,128)S(1)}, f32[3,8,1024]{2,1,0:T(8,128)S(1)}, u32[]{:S(2)}, u32[]{:S(2)}) collective-permute-start(f32[3,8,1024]{2,1,0:T(8,128)S(1)} %slice.9), channel_id=1, source_target_pairs={{0,4},{4,8},{8,12},{12,16},{16,20},{20,24},{24,28},{28,32},{32,36}... | collective-permute-start | bytes 294920 | tf_op jit(solution)/shard_map/ppermute | solution.py:355
  7.1 0.6 copy-start.4
  7.7 3.0 %copy-start.7 = (f32[4,128]{1,0:T(4,128)S(1)}, f32[4,128]{1,0:T(4,128)}, u32[]{:S(2)}) copy-start(f32[4,128]{1,0:T(4,128)} %param.11) | copy-start | bytes 6148
  11.4 14.7 %all-to-all-start.1 = ((f32[8,1,128]{2,1,0:T(1,128)}), f32[8,1,128]{2,1,0:T(1,128)S(1)}, u32[]{:S(2)}, u32[]{:S(2)}) async-start(f32[8,1,128]{2,1,0:T(1,128)} %bitcast.3), calls=%async_computation.1 | async-start | bytes 8192 | tf_op jit(solution)/shard_map/all_to_all | solution.py:371
  24.7 15.5 %copy-start.8 = (f32[32,1,4,8,128]{4,3,2,1,0:T(8,128)S(1)}, f32[32,1,4,8,128]{4,3,2,1,0:T(8,128)}, u32[]{:S(2)}) copy-start(f32[32,1,4,8,128]{4,3,2,1,0:T(8,128)} %get-tuple-element.25) | copy-start | bytes 1572868
  26.1 42.7 %all-to-all-start = ((f32[32,2,4,8,128]{4,3,2,1,0:T(8,128)}), f32[32,2,4,8,128]{4,3,2,1,0:T(8,128)S(1)}, u32[]{:S(2)}, u32[]{:S(2)}) async-start(f32[32,2,4,8,128]{4,3,2,1,0:T(8,128)} %get-tuple-element.28), calls=%async_computation | async-start | bytes 2097152 | tf_op jit(solution)/shard_map/all_to_all | solution.py:347
  40.3 28.6 %collective-permute-start.1 = (f32[32,1,4,8,128]{4,3,2,1,0:T(8,128)S(1)}, f32[32,1,4,8,128]{4,3,2,1,0:T(8,128)S(1)}, u32[]{:S(2)}, u32[]{:S(2)}) collective-permute-start(f32[32,1,4,8,128]{4,3,2,1,0:T(8,128)S(1)} %copy-done.8), channel_id=1, source_target_pairs={{0,32},{32,0},{1,33},{33,1},{2,34},{34,2},{3,35},{35,3},{4,36},{36... | collective-permute-start | bytes 1572872 | tf_op jit(solution)/shard_map/ppermute | solution.py:343
  68.8 10.7 %copy-start.2 = (f32[32,2,4,8,128]{4,3,2,1,0:T(8,128)}, f32[32,2,4,8,128]{4,3,2,1,0:T(8,128)S(1)}, u32[]{:S(2)}) copy-start(f32[32,2,4,8,128]{4,3,2,1,0:T(8,128)S(1)} %all-to-all-done) | copy-start | bytes 3145732
  71.4 26.5 %all-to-all-start.2 = ((f32[32,72,128]{2,1,0:T(8,128)}), f32[32,72,128]{2,1,0:T(8,128)S(1)}, u32[]{:S(2)}, u32[]{:S(2)}) async-start(f32[32,72,128]{2,1,0:T(8,128)} %pad_maximum_fusion), calls=%async_computation.2 | async-start | bytes 2359296 | tf_op jit(solution)/shard_map/all_to_all | solution.py:347
  79.6 29.7 %collective-permute-start.3 = (f32[32,4,8,128]{3,2,1,0:T(8,128)S(1)}, f32[32,4,8,128]{3,2,1,0:T(8,128)S(1)}, u32[]{:S(2)}, u32[]{:S(2)}) collective-permute-start(f32[32,4,8,128]{3,2,1,0:T(8,128)S(1)} %slice_bitcast_fusion.1), channel_id=1, source_target_pairs={{0,32},{32,0},{1,33},{33,1},{2,34},{34,2},{3,35},{35,3},{4,36},{36... | collective-permute-start | bytes 1572872 | tf_op jit(solution)/shard_map/ppermute | solution.py:343
  97.9 1.0 copy-start.3
  109.3 0.8 copy-start.10
  120.2 4.1 %copy-start.9 = (f32[1024,128]{1,0:T(8,128)S(1)}, f32[1024,128]{1,0:T(8,128)}, u32[]{:S(2)}) copy-start(f32[1024,128]{1,0:T(8,128)} %get-tuple-element.32) | copy-start | bytes 1572868
  120.2 27.5 %copy-start.5 = (f32[1024,128]{1,0:T(8,128)S(1)}, f32[1024,128]{1,0:T(8,128)}, u32[]{:S(2)}) copy-start(f32[1024,128]{1,0:T(8,128)} %get-tuple-element.39) | copy-start | bytes 1572868
  120.2 27.5 %all-to-all-start.3 = ((f32[32,2,4,8,128]{4,3,2,1,0:T(8,128)}), f32[32,2,4,8,128]{4,3,2,1,0:T(8,128)S(1)}, u32[]{:S(2)}, u32[]{:S(2)}) async-start(f32[32,2,4,8,128]{4,3,2,1,0:T(8,128)} %bitcast.21), calls=%async_computation.3 | async-start | bytes 2097152 | tf_op jit(solution)/shard_map/all_to_all | solution.py:347
  124.3 23.5 %collective-permute-start.2 = (f32[1024,128]{1,0:T(8,128)S(1)}, f32[1024,128]{1,0:T(8,128)S(1)}, u32[]{:S(2)}, u32[]{:S(2)}) collective-permute-start(f32[1024,128]{1,0:T(8,128)S(1)} %copy-done.9), channel_id=1, source_target_pairs={{0,32},{32,0},{1,33},{33,1},{2,34},{34,2},{3,35},{35,3},{4,36},{36... | collective-permute-start | bytes 1572872 | tf_op jit(solution)/shard_map/ppermute | solution.py:343
  147.7 8.7 %copy-start.1 = (f32[32,2,4,8,128]{4,3,2,1,0:T(8,128)}, f32[32,2,4,8,128]{4,3,2,1,0:T(8,128)S(1)}, u32[]{:S(2)}) copy-start(f32[32,2,4,8,128]{4,3,2,1,0:T(8,128)S(1)} %all-to-all-done.3.long_ref) | copy-start | bytes 3145732
  148.9 24.4 %all-to-all-start.4 = ((f32[32,2,4,8,128]{4,3,2,1,0:T(8,128)}), f32[32,2,4,8,128]{4,3,2,1,0:T(8,128)S(1)}, u32[]{:S(2)}, u32[]{:S(2)}) async-start(f32[32,2,4,8,128]{4,3,2,1,0:T(8,128)} %maximum_bitcast_fusion), calls=%async_computation.4 | async-start | bytes 2097152 | tf_op jit(solution)/shard_map/all_to_all | solution.py:347
  156.5 22.2 %collective-permute-start.4 = (f32[32,4,8,128]{3,2,1,0:T(8,128)S(1)}, f32[32,4,8,128]{3,2,1,0:T(8,128)S(1)}, u32[]{:S(2)}, u32[]{:S(2)}) collective-permute-start(f32[32,4,8,128]{3,2,1,0:T(8,128)S(1)} %slice_bitcast_fusion), channel_id=1, source_target_pairs={{0,32},{32,0},{1,33},{33,1},{2,34},{34,2},{3,35},{35,3},{4,36},{36... | collective-permute-start | bytes 1572872 | tf_op jit(solution)/shard_map/ppermute | solution.py:343
  173.3 1.0 copy-start
  178.7 0.8 copy-start.6

commit v2 on v1

v2 whole, which is shorter than its diff:
```python
import functools

import jax
import jax.numpy as jnp
import ml_dtypes
import numpy as np
from jax import lax
from jax.experimental import pallas as pl
from jax.experimental.pallas import tpu as pltpu
from jax.sharding import Mesh
from jax.sharding import PartitionSpec as P

f32 = jnp.float32
bf16 = jnp.bfloat16

ROWS = 512
TAPS = 7
LANES = 128
PEERS = 32
PIECE = 8
QUARTERS = ROWS // LANES
BLOCK = QUARTERS * PIECE
HALF = PEERS * BLOCK
LENGTH = 32768
VMEM_BYTES = 16 << 20
CONV_BYTES = 40 << 20
SLOW = 200_000
ORDER = 256

SEQ = ("x", "zh", "y", "core")
PLANE = ("x", "y", "core")


def split_np(table):
    high = table.astype(np.float32).astype(ml_dtypes.bfloat16)
    low = (table - high.astype(np.float64)).astype(ml_dtypes.bfloat16)
    return high, low


def position_blocks():
    n1 = np.zeros((2, 4, PEERS), np.int64)
    for z in range(2):
        for q in range(4):
            for p in range(PEERS):
                x, rest = divmod(p, 8)
                n1[z, q, p] = 4 * (x * 16 + z * 8 + rest) + q
    return n1.reshape(-1)


def make_tables():
    n1 = position_blocks()
    k1 = np.arange(ORDER)
    m = np.arange(LANES)
    turn = 2.0 * np.pi
    first = turn * (((4 * k1[:, None] + 1) * n1[None, :]) % (4 * ORDER)) / (4 * ORDER)
    first = np.concatenate([np.cos(first), -np.sin(first)], axis=0)
    bend = turn * ((4 * k1[:, None] + 1) * m[None, :]) / (4 * LENGTH)
    second = turn * ((m[:, None] * m[None, :]) % LANES) / LANES
    cosine, sine = np.cos(second), np.sin(second)
    onward = np.block([[cosine, -sine], [sine, cosine]])
    back = np.block([[cosine, sine], [-sine, cosine]])
    last = first.T
    first_high, first_low = split_np(first)
    onward_high, onward_low = split_np(onward)
    back_high, back_low = split_np(back)
    last_high, last_low = split_np(last)
    return dict(
        first=np.concatenate([first_high, first_low], axis=1),
        last=np.concatenate([last_high, last_low], axis=1),
        onward=np.concatenate([onward_high, onward_low], axis=0),
        back=np.concatenate([back_high, back_low], axis=0),
        bend=np.stack([np.cos(bend), -np.sin(bend)]).astype(np.float32),
    )


def halves(x):
    high = x.astype(bf16)
    low = (x - high.astype(f32)).astype(bf16)
    return high, low


def thrice(table, axis):
    half = table.shape[axis] // 2
    high = lax.slice_in_dim(table, 0, half, axis=axis)
    return jnp.concatenate([high, table], axis=axis)


def dot(a, b):
    return jnp.dot(a, b, preferred_element_type=f32)


def to_spectrum(columns, first, onward, bend):
    high, low = halves(columns)
    section = dot(first, jnp.concatenate([high, low, high], axis=0))
    bend_re, bend_im = bend[0], bend[1]
    rows = []
    for at in range(columns.shape[1] // LANES):
        re = section[:ORDER, at * LANES : (at + 1) * LANES]
        im = section[ORDER:, at * LANES : (at + 1) * LANES]
        rows.append(
            jnp.concatenate([re * bend_re - im * bend_im, re * bend_im + im * bend_re], axis=1)
        )
    bent = jnp.concatenate(rows, axis=0)
    high, low = halves(bent)
    return dot(jnp.concatenate([high, low, high], axis=1), onward)


def from_spectrum(spectrum, last, back, bend):
    high, low = halves(spectrum)
    section = dot(jnp.concatenate([high, low, high], axis=1), back)
    bend_re, bend_im = bend[0], bend[1]
    columns = []
    for at in range(spectrum.shape[0] // ORDER):
        re = section[at * ORDER : (at + 1) * ORDER, :LANES]
        im = section[at * ORDER : (at + 1) * ORDER, LANES:]
        columns.append(
            jnp.concatenate([re * bend_re + im * bend_im, im * bend_re - re * bend_im], axis=0)
        )
    bent = jnp.concatenate(columns, axis=1)
    high, low = halves(bent)
    return dot(last, jnp.concatenate([high, low, high], axis=0))


def pieces_of(source_ref, target_ref, count):
    count = min(count, source_ref.shape[0])
    rows = source_ref.shape[0] // count
    cuts = [pl.ds(at * rows, rows) for at in range(count)]
    return [(source_ref.at[cut], target_ref.at[cut]) for cut in cuts]


def copies_of(pairs, sems):
    copies = [
        pltpu.make_async_copy(source, target, sems.at[at])
        for at, (source, target) in enumerate(pairs)
    ]
    for copy in copies:
        copy.start()
    return copies


def wait_all(copies):
    for copy in copies:
        copy.wait()


CUTS = 1


BATCH = 2
LAG = 1


def pieces_taps(ref, at, stride):
    return jnp.concatenate([ref[pl.ds(at + zq, PEERS, stride=stride), :] for zq in range(8)], axis=0)


def conv_kernel(layout, sources, outputs, after, z_ref, *refs):
    own_at, own_stride, other_at, other_stride, taps_at = layout
    inputs = sources + 5
    given, results = refs[:inputs], refs[inputs + after : inputs + after + outputs]
    held = refs[inputs + after + outputs : -2]
    in_sems, out_sems = refs[-2:]
    order = list(range(sources)) + [sources + at for at in (0, 4, 2, 3, 1)]
    arrivals = {}
    for k in order:
        arrivals[k] = copies_of(pieces_of(given[k], held[k], CUTS), in_sems.at[k])
    own_ref, other_ref, spectrum_ref = (held[:sources] * 3)[:3]
    first_ref, last_ref, onward_ref, back_ref, bend_ref = held[sources:inputs]
    out_refs = held[inputs:]
    low_plane = z_ref[0] == 0
    wide = 2 * BLOCK if outputs == 1 else BLOCK

    for k in range(sources):
        wait_all(arrivals[k])
    extra = [pieces_taps(spectrum_ref, taps_at, own_stride)] if taps_at is not None else []
    wait_all(arrivals[sources] + arrivals[sources + 4] + arrivals[sources + 2])
    bend = bend_ref[...]
    bend_re, bend_im = bend[0], bend[1]
    leaving = []
    if taps_at is not None:
        taps = to_spectrum(extra[0], thrice(first_ref[...], 1), thrice(onward_ref[...], 0), bend) * (1.0 / LENGTH)
        out_refs[2][...] = taps
        leaving = copies_of(pieces_of(out_refs[2], results[2], 1), out_sems.at[2])
    else:
        taps = spectrum_ref[...]
    taps_re = taps[:, :LANES]
    taps_im = taps[:, LANES:]

    def gather(at):
        own, other = [], []
        for q in range(4):
            row = q * PIECE + at
            own.append(own_ref[pl.ds(own_at + row, PEERS, stride=own_stride), :])
            other.append(other_ref[pl.ds(other_at + row, PEERS, stride=other_stride), :])
        own = jnp.concatenate(own, axis=0)
        other = jnp.concatenate(other, axis=0)
        return jnp.concatenate(
            [jnp.where(low_plane, own, other), jnp.where(low_plane, other, own)], axis=0
        )

    def store(at, column):
        upper, lower = column[: ORDER // 2], column[ORDER // 2 :]
        own = jnp.where(low_plane, upper, lower)
        other = jnp.where(low_plane, lower, upper)
        for q in range(4):
            row = q * PIECE + at
            rows_own = own[q * PEERS : (q + 1) * PEERS]
            rows_other = other[q * PEERS : (q + 1) * PEERS]
            out_refs[0][pl.ds(row, PEERS, stride=wide), :] = rows_own
            if outputs == 1:
                out_refs[0][pl.ds(BLOCK + row, PEERS, stride=2 * BLOCK), :] = rows_other
            else:
                out_refs[1][pl.ds(row, PEERS, stride=BLOCK), :] = rows_other

    def load(channels):
        high, low = halves(jnp.concatenate([gather(at) for at in channels], axis=1))
        return jnp.concatenate([high, low, high], axis=0)

    def to_blocks(x):
        return dot(thrice(first_ref[...], 1), x)

    def bend_onward(section):
        rows = []
        for at in range(section.shape[1] // LANES):
            re = section[:ORDER, at * LANES : (at + 1) * LANES]
            im = section[ORDER:, at * LANES : (at + 1) * LANES]
            rows.append(
                jnp.concatenate([re * bend_re - im * bend_im, re * bend_im + im * bend_re], axis=1)
            )
        high, low = halves(jnp.concatenate(rows, axis=0))
        return jnp.concatenate([high, low, high], axis=1)

    def to_frequencies(x):
        return dot(x, thrice(onward_ref[...], 0))

    def weigh(spectrum):
        rows = []
        for at in range(spectrum.shape[0] // ORDER):
            re = spectrum[at * ORDER : (at + 1) * ORDER, :LANES]
            im = spectrum[at * ORDER : (at + 1) * ORDER, LANES:]
            rows.append(
                jnp.concatenate([re * taps_re - im * taps_im, re * taps_im + im * taps_re], axis=1)
            )
        high, low = halves(jnp.concatenate(rows, axis=0))
        return jnp.concatenate([high, low, high], axis=1)

    def from_frequencies(x):
        return dot(x, thrice(back_ref[...], 0))

    def bend_back(section):
        columns = []
        for at in range(section.shape[0] // ORDER):
            re = section[at * ORDER : (at + 1) * ORDER, :LANES]
            im = section[at * ORDER : (at + 1) * ORDER, LANES:]
            columns.append(
                jnp.concatenate([re * bend_re + im * bend_im, im * bend_re - re * bend_im], axis=0)
            )
        high, low = halves(jnp.concatenate(columns, axis=1))
        return jnp.concatenate([high, low, high], axis=0)

    def from_blocks(x):
        return dot(thrice(last_ref[...], 1), x)

    stages = (
        load, to_blocks, bend_onward, to_frequencies, weigh, from_frequencies, bend_back, from_blocks
    )
    batches = [tuple(range(at, at + BATCH)) for at in range(0, PIECE, BATCH)]
    state = list(batches)
    for tick in range(len(stages) + 1 + LAG * (len(batches) - 1)):
        if tick == 5:
            wait_all(arrivals[sources + 3] + arrivals[sources + 1])
        for batch, channels in enumerate(batches):
            stage = tick - LAG * batch
            if 0 <= stage < len(stages):
                state[batch] = stages[stage](state[batch])
            elif stage == len(stages):
                for at, channel in enumerate(channels):
                    store(channel, state[batch][:, at * LANES : (at + 1) * LANES])
    for k in range(min(outputs, 2)):
        leaving = leaving + copies_of(pieces_of(out_refs[k], results[k], CUTS), out_sems.at[k])
    wait_all(leaving)


def short_sum(short, long_ref, at, step):
    total = short[0:1] * long_ref[at + 2 : at + 2 + step, :]
    for i in range(1, TAPS):
        total = total + short[i : i + 1] * long_ref[at + 2 + i : at + 2 + i + step, :]
    return total


def fetch(proj_ref, halo_ref, short_ref, buffer_ref, halo_held, taps_held, sems, streams, columns):
    edges = copies_of([(halo_ref, halo_held), (short_ref, taps_held)], sems.at[len(columns)])
    first, count = streams
    blocks = []
    for i, column in enumerate(columns):
        lanes = pl.ds(pl.multiple_of(column, LANES), LANES)
        copy = pltpu.make_async_copy(
            proj_ref.at[pl.ds(first, count), :, lanes],
            buffer_ref.at[i, :, pl.ds(8, ROWS)],
            sems.at[i, 0],
        )
        copy.start()
        blocks.append(copy)
    wait_all(edges)
    for i, column in enumerate(columns):
        lanes = pl.ds(pl.multiple_of(column, LANES), LANES)
        buffer_ref[i, :, 0:8, :] = halo_held[first : first + count, :, lanes]
    return blocks


def feature_kernel(columns_of_z, z_ref, halo_ref, short_ref, proj_ref, *rest):
    sent_ref, product_ref = rest[-9:-7]
    buffer_ref, halo_held, taps_held, sems, out_sems, turned_ref, flat_ref = rest[-7:]
    step = 64
    columns = columns_of_z(z_ref[0])
    blocks = fetch(
        proj_ref, halo_ref, short_ref, buffer_ref, halo_held, taps_held, sems, (1, 2), columns
    )
    peers = LANES // PIECE
    leaving = []
    for i, copy in enumerate(blocks):
        copy.wait()
        lanes = pl.ds(pl.multiple_of(columns[i], LANES), LANES)
        key_taps, value_taps = taps_held[1, :, lanes], taps_held[2, :, lanes]
        for quarter in range(QUARTERS):
            parts = []
            for at in range(quarter * LANES, (quarter + 1) * LANES, step):
                product = short_sum(key_taps, buffer_ref.at[i, 0], at, step) * short_sum(
                    value_taps, buffer_ref.at[i, 1], at, step
                )
                flat_ref[i, at : at + step, :] = product
                parts.append(product)
            turned = jnp.concatenate(parts, axis=0).T
            turned_ref[i, :, quarter] = turned.reshape(peers, PIECE, LANES)
        into = sent_ref.at[
            pl.ds(i % 2 * peers, peers), pl.ds(i // 2 * QUARTERS, QUARTERS)
        ]
        pairs = [(turned_ref.at[i], into)]
        pairs.append((flat_ref.at[i], product_ref.at[:, pl.ds(i * LANES, LANES)]))
        leaving = leaving + copies_of(pairs, out_sems.at[i])
    wait_all(leaving)


def gate_kernel(z_ref, halo_ref, short_ref, proj_ref, *rest):
    gate_ref, buffer_ref, halo_held, taps_held, sems, out_sems, flat_ref = rest[-7:]
    step = 64
    columns = [i * LANES for i in range(8)]
    blocks = fetch(
        proj_ref, halo_ref, short_ref, buffer_ref, halo_held, taps_held, sems, (0, 1), columns
    )
    leaving = []
    for i, copy in enumerate(blocks):
        copy.wait()
        taps = taps_held[0, :, i * LANES : (i + 1) * LANES]
        for at in range(0, ROWS, step):
            flat_ref[i, at : at + step, :] = short_sum(taps, buffer_ref.at[i, 0], at, step)
        pairs = [(flat_ref.at[i], gate_ref.at[:, pl.ds(i * LANES, LANES)])]
        leaving = leaving + copies_of(pairs, out_sems.at[i])
    wait_all(leaving)


def final_kernel(z_ref, long_ref, gate_ref, product_ref, skip_ref, *rest):
    out_ref = rest[-1]
    skip = skip_ref[0:1, :]
    for start in range(0, ROWS, LANES):
        rows = slice(start, start + LANES)
        turned = long_ref[:, start // LANES].reshape(LANES, LANES).T
        out_ref[rows, :] = gate_ref[rows, :] * (turned + skip * product_ref[rows, :])


def columns_of(chunk, slots):
    def column(i, z_ref):
        plane = z_ref[0]
        if slots == (1,):
            plane = 1 - plane
        elif len(slots) == 2:
            plane = jnp.where(i // 2 == 0, plane, 1 - plane)
        return plane * 2 + i % 2 + chunk * 4

    return column


def from_streams(kernel, streams, blocks, extra, out_shape, weight, z, projected, halo, short_filter, after):
    return pl.pallas_call(
        kernel,
        in_specs=[
            pl.BlockSpec(memory_space=pltpu.SMEM),
            pl.BlockSpec(memory_space=pl.ANY),
            pl.BlockSpec(memory_space=pltpu.HBM),
            pl.BlockSpec(memory_space=pltpu.HBM),
        ]
        + [pl.BlockSpec(memory_space=pl.ANY)] * len(after),
        out_specs=[pl.BlockSpec(memory_space=pl.ANY)] * len(out_shape),
        out_shape=out_shape,
        scratch_shapes=[
            pltpu.VMEM((blocks, streams, ROWS + 8, LANES), f32),
            pltpu.VMEM(halo.shape, f32),
            pltpu.VMEM(short_filter.shape, f32),
            pltpu.SemaphoreType.DMA((blocks + 1, 2)),
            pltpu.SemaphoreType.DMA((blocks, 2)),
        ]
        + extra,
        compiler_params=pltpu.CompilerParams(vmem_limit_bytes=VMEM_BYTES),
        cost_estimate=pl.CostEstimate(
            flops=weight * 1_000_000, bytes_accessed=1_000_000, transcendentals=0
        ),
        name="streams",
    )(z, halo, short_filter, projected, *after)


def features_of(z, chunk, slots, projected, halo, short_filter, after=(), weight=1):
    count = len(slots)
    blocks = 2 * count

    def columns_of_z(plane):
        planes = [plane if slot == 0 else 1 - plane for slot in slots for _ in range(2)]
        return [(chunk * 4 + planes[i] * 2 + i % 2) * LANES for i in range(blocks)]

    out_shape = [
        jax.ShapeDtypeStruct((PEERS, count * QUARTERS, PIECE, LANES), f32),
        jax.ShapeDtypeStruct((ROWS, blocks * LANES), f32),
    ]
    kernel = functools.partial(feature_kernel, columns_of_z)
    extra = [
        pltpu.VMEM((blocks, LANES // PIECE, QUARTERS, PIECE, LANES), f32),
        pltpu.VMEM((blocks, ROWS, LANES), f32),
    ]
    return from_streams(
        kernel, 2, blocks, extra, out_shape, weight, z, projected, halo, short_filter, after
    )


def gates_of(z, projected, halo, short_filter, after):
    out_shape = [jax.ShapeDtypeStruct((ROWS, 8 * LANES), f32)]
    return from_streams(
        gate_kernel, 1, 8, [pltpu.VMEM((8, ROWS, LANES), f32)], out_shape, SLOW, z, projected, halo, short_filter, after
    )[0]


def finish_own(z, b_out, gate, product_b, skip):
    column = columns_of(1, (0,))
    return pl.pallas_call(
        final_kernel,
        grid_spec=pltpu.PrefetchScalarGridSpec(
            num_scalar_prefetch=1,
            grid=(2,),
            in_specs=[
                pl.BlockSpec((LANES // PIECE, QUARTERS, PIECE, LANES), lambda i, z: (i, 0, 0, 0)),
                pl.BlockSpec((ROWS, LANES), lambda i, z: (0, column(i, z))),
                pl.BlockSpec((ROWS, LANES), lambda i, z: (0, i)),
                pl.BlockSpec((1, LANES), lambda i, z: (0, column(i, z))),
            ],
            out_specs=pl.BlockSpec((ROWS, LANES), lambda i, z: (0, column(i, z))),
        ),
        out_shape=jax.ShapeDtypeStruct((ROWS, 8 * LANES), f32),
        compiler_params=pltpu.CompilerParams(vmem_limit_bytes=VMEM_BYTES),
        cost_estimate=pl.CostEstimate(
            flops=SLOW * 1_000_000, bytes_accessed=1_000_000, transcendentals=0
        ),
        name="finish",
    )(z, b_out, gate, product_b, skip)


def finish_rest_kernel(
    z_ref,
    a_ref,
    b_ref,
    gate_ref,
    own_ref,
    other_ref,
    b_product_ref,
    skip_ref,
    whole_ref,
    out_ref,
    long_vmem,
    gate_vmem,
    product_vmem,
    out_vmem,
    in_sems,
    out_sems,
):
    z = z_ref[0]
    places = []
    arrivals = []
    for i in range(3):
        plane = z if i == 0 else 1 - z
        column = pl.multiple_of(((0 if i < 2 else 4) + plane * 2) * LANES, 2 * LANES)
        lanes = pl.ds(column, 2 * LANES)
        places.append(lanes)
        product = (own_ref, other_ref, b_product_ref)[i]
        flat = pl.ds((2 if i == 2 else 0) * LANES, 2 * LANES)
        pairs = [
            (a_ref.at[:, pl.ds(QUARTERS * i, QUARTERS)] if i < 2 else b_ref, long_vmem.at[i]),
            (gate_ref.at[:, lanes], gate_vmem.at[i]),
            (product.at[:, flat], product_vmem.at[i]),
        ]
        arrivals.append(copies_of(pairs, in_sems.at[i]))
    leaving = []
    for i in range(3):
        wait_all(arrivals[i])
        skip = skip_ref[0:1, places[i]]
        for quarter in range(QUARTERS):
            rows = slice(quarter * LANES, (quarter + 1) * LANES)
            turned = long_vmem[i, :, quarter].reshape(2 * LANES, LANES).T
            out_vmem[i, rows, :] = gate_vmem[i, rows, :] * (
                turned + skip * product_vmem[i, rows, :]
            )
        leaving = leaving + copies_of(
            [(out_vmem.at[i], out_ref.at[:, places[i]])], out_sems.at[i]
        )
    wait_all(leaving)


def finish_rest(z, a_out, b_back, gate, product_a, product_ao, product_b, skip, whole):
    operands = [z, a_out, b_back, gate, product_a, product_ao, product_b, skip, whole]
    anywhere = pl.BlockSpec(memory_space=pl.ANY)
    flat = pltpu.VMEM((3, ROWS, 2 * LANES), f32)
    return pl.pallas_call(
        finish_rest_kernel,
        in_specs=[pl.BlockSpec(memory_space=pltpu.SMEM)]
        + [anywhere] * 6
        + [pl.BlockSpec(memory_space=pltpu.VMEM), anywhere],
        out_specs=anywhere,
        out_shape=jax.ShapeDtypeStruct((ROWS, 8 * LANES), f32),
        scratch_shapes=[
            pltpu.VMEM((3, PEERS, QUARTERS, PIECE, LANES), f32),
            flat,
            flat,
            flat,
            pltpu.SemaphoreType.DMA((3, 3)),
            pltpu.SemaphoreType.DMA((3, 1)),
        ],
        input_output_aliases={len(operands) - 1: 0},
        compiler_params=pltpu.CompilerParams(vmem_limit_bytes=CONV_BYTES),
        cost_estimate=pl.CostEstimate(
            flops=1_000_000, bytes_accessed=1_000_000, transcendentals=0
        ),
        name="finish",
    )(*operands)


def convolve(z, layout, sources, tables, joined, after=()):
    if joined:
        out_shape = [jax.ShapeDtypeStruct((2 * HALF, LANES), f32)]
    else:
        out_shape = [
            jax.ShapeDtypeStruct((HALF, LANES), f32),
            jax.ShapeDtypeStruct((HALF, LANES), f32),
            jax.ShapeDtypeStruct((ORDER, 2 * LANES), f32),
        ]
    operands = list(sources) + [
        in_hbm(tables[name]) for name in ("first", "last", "onward", "back", "bend")
    ]
    anywhere = pl.BlockSpec(memory_space=pl.ANY)
    shapes = [(x.shape, x.dtype) for x in operands + out_shape]
    return pl.pallas_call(
        functools.partial(conv_kernel, layout, len(sources), len(out_shape), len(after)),
        in_specs=[pl.BlockSpec(memory_space=pltpu.SMEM)]
        + [anywhere] * (len(operands) + len(after)),
        out_specs=[anywhere] * len(out_shape),
        out_shape=out_shape,
        scratch_shapes=[pltpu.VMEM(shape, dtype) for shape, dtype in shapes]
        + [
            pltpu.SemaphoreType.DMA((len(operands), CUTS)),
            pltpu.SemaphoreType.DMA((len(out_shape), CUTS)),
        ],
        compiler_params=pltpu.CompilerParams(vmem_limit_bytes=CONV_BYTES),
        cost_estimate=pl.CostEstimate(
            flops=10_000_000, bytes_accessed=1_000_000, transcendentals=0
        ),
        name="convolve",
    )(z, *operands, *after)


def in_hbm(x):
    return pltpu.with_memory_space_constraint(x, pltpu.HBM)


def swap_planes(x):
    return lax.ppermute(x, "zh", [(0, 1), (1, 0)])


def across(x):
    return lax.all_to_all(x, PLANE, split_axis=0, concat_axis=0, tiled=True)


def relay(pairs, held_refs, in_sems, out_sems):
    arrivals, targets = [], []
    for at, ((source, target), held) in enumerate(zip(pairs, held_refs)):
        arrivals.append(copies_of(pieces_of(source, held, CUTS), in_sems.at[at]))
        targets.append(pieces_of(held, target, CUTS))
    leaving = []
    for cut in range(CUTS):
        for at in range(len(pairs)):
            arrivals[at][cut].wait()
            source, target = targets[at][cut]
            copy = pltpu.make_async_copy(source, target, out_sems.at[at, cut])
            copy.start()
            leaving.append(copy)
    return leaving


def join_taps_kernel(
    place_ref,
    own_ref,
    from_ref,
    here_ref,
    there_ref,
    after_ref,
    out_ref,
    own_held,
    from_held,
    in_sems,
    out_sems,
    taps_held,
    small_held,
    small_sems,
):
    pairs = [
        (own_ref, out_ref.at[:, pl.ds(0, QUARTERS)]),
        (from_ref, out_ref.at[:, pl.ds(QUARTERS, QUARTERS)]),
    ]
    small = [(here_ref, small_held.at[0]), (there_ref, small_held.at[1])]
    wait_all(copies_of(small, small_sems))
    leaving = relay(pairs, (own_held, from_held), in_sems, out_sems)
    z, group = place_ref[0], place_ref[1]
    for zq in range(8):
        row = (jnp.bitwise_xor(zq % 4, group) * 4) + group
        here = small_held[0, pl.ds(row, 1), :]
        there = small_held[1, pl.ds(row, 1), :]
        taps = jnp.where(z == zq // 4, here, there)
        taps_held[:, 0, zq : zq + 1, :] = jnp.broadcast_to(taps[None], (PEERS, 1, LANES))
    into = out_ref.at[:, pl.ds(2 * QUARTERS, 1)]
    wait_all(leaving + copies_of([(taps_held, into)], small_sems))


def join_kernel(own_ref, from_ref, after_ref, out_ref, own_held, from_held, in_sems, out_sems):
    pairs = [
        (own_ref, out_ref.at[:, pl.ds(0, QUARTERS)]),
        (from_ref, out_ref.at[:, pl.ds(QUARTERS, QUARTERS)]),
    ]
    wait_all(relay(pairs, (own_held, from_held), in_sems, out_sems))


def cut_kernel(both_ref, after_ref, out_ref, held, in_sems, out_sems):
    pairs = [(both_ref.at[:, pl.ds(QUARTERS, QUARTERS)], out_ref)]
    wait_all(relay(pairs, (held,), in_sems, out_sems))


def token_kernel(after_ref, out_ref):
    pass


def rearrange(kernel, operands, groups, pieces, place=None, cost=1_000):
    anywhere = pl.BlockSpec(memory_space=pl.ANY)
    scratch = [pltpu.VMEM((PEERS, QUARTERS, PIECE, LANES), f32)] * pieces
    scratch = scratch + [pltpu.SemaphoreType.DMA((pieces, CUTS))] * 2
    in_specs = [anywhere] * len(operands)
    if place is not None:
        scratch.append(pltpu.VMEM((PEERS, 1, PIECE, LANES), f32))
        scratch.append(pltpu.VMEM((2, 16, LANES), f32))
        scratch.append(pltpu.SemaphoreType.DMA((2,)))
        in_specs = [pl.BlockSpec(memory_space=pltpu.SMEM)] + in_specs
        operands = (place, *operands)
    return pl.pallas_call(
        kernel,
        in_specs=in_specs,
        out_specs=anywhere,
        out_shape=jax.ShapeDtypeStruct((PEERS, groups, PIECE, LANES), f32),
        scratch_shapes=scratch,
        compiler_params=pltpu.CompilerParams(vmem_limit_bytes=VMEM_BYTES),
        cost_estimate=pl.CostEstimate(flops=cost, bytes_accessed=1_000, transcendentals=0),
        name="rearrange",
    )(*operands)


def token(after):
    anywhere = pl.BlockSpec(memory_space=pl.ANY)
    return pl.pallas_call(
        token_kernel,
        in_specs=[anywhere],
        out_specs=anywhere,
        out_shape=jax.ShapeDtypeStruct((8, LANES), f32),
        cost_estimate=pl.CostEstimate(
            flops=SLOW * 1_000_000, bytes_accessed=1_000, transcendentals=0
        ),
        name="token",
    )(after)


def later_kernel(*refs):
    for at in range(4):
        refs[-1][at * 4 : (at + 1) * 4] = refs[at][...]


def later_rows(parts, after):
    inside = pl.BlockSpec(memory_space=pltpu.VMEM)
    return pl.pallas_call(
        later_kernel,
        in_specs=[inside] * 4 + [pl.BlockSpec(memory_space=pl.ANY)],
        out_specs=inside,
        out_shape=jax.ShapeDtypeStruct((16, LANES), f32),
        cost_estimate=pl.CostEstimate(flops=1_000, bytes_accessed=1_000, transcendentals=0),
        name="later",
    )(*parts, after)


def body(projected, short_filter, long_filter, skip_gain):
    tables = {name: jnp.asarray(table) for name, table in make_tables().items()}
    z = lax.axis_index("zh").astype(jnp.int32).reshape(1)
    skip = skip_gain.reshape(1, -1)
    devices = lax.axis_size(SEQ)
    halo = lax.ppermute(
        projected[:, ROWS - 8 :, :], SEQ, [(i, i + 1) for i in range(devices - 1)]
    )
    projected, short_filter = in_hbm(projected), in_hbm(short_filter)
    feature = functools.partial(
        features_of, projected=projected, halo=halo, short_filter=short_filter
    )
    a_other, product_ao = feature(z, 0, (1,))
    a_from = swap_planes(a_other)
    b_both, product_b = feature(z, 1, (0, 1), after=(product_ao,))
    b_here = across(b_both)
    a_own, product_a = feature(z, 0, (0,), after=(product_b,), weight=SLOW)

    steps = [
        lax.ppermute(long_filter, "zl", [(i, i ^ d) for i in range(4)]) for d in range(1, 4)
    ]
    taps_here = later_rows((long_filter, *steps), a_own)
    taps_there = swap_planes(taps_here)
    group = lax.axis_index("zl").astype(jnp.int32).reshape(1)
    place = jnp.concatenate([z, group])

    b_sent = rearrange(cut_kernel, (in_hbm(b_here), a_from), QUARTERS, 1)
    b_from = swap_planes(b_sent)
    a_sent = rearrange(
        join_taps_kernel,
        (in_hbm(a_own), a_from, taps_here, taps_there, in_hbm(b_sent)),
        2 * QUARTERS + 1,
        2,
        place=place,
        cost=10_000_000_000,
    )
    a_here = across(a_sent)
    gate = gates_of(z, projected, halo, short_filter, (a_from, b_here))
    wide = 2 * BLOCK + 8
    conv_a_own, conv_a_other, spectrum = convolve(
        z,
        (0, wide, BLOCK, wide, 2 * BLOCK),
        (in_hbm(a_here.reshape(-1, LANES)),),
        tables,
        False,
        (gate,),
    )

    a_back = swap_planes(conv_a_other.reshape(PEERS, QUARTERS, PIECE, LANES))
    (conv_b,) = convolve(
        z,
        (0, 2 * BLOCK, 0, BLOCK, None),
        (in_hbm(b_here.reshape(2 * HALF, LANES)), b_from.reshape(HALF, LANES), spectrum),
        tables,
        True,
    )
    b_out = across(conv_b.reshape(PEERS, 2 * QUARTERS, PIECE, LANES))

    a_kept = in_hbm(conv_a_own.reshape(PEERS, QUARTERS, PIECE, LANES))
    b_sent = rearrange(cut_kernel, (in_hbm(b_out), in_hbm(token(a_back))), QUARTERS, 1)
    b_back = swap_planes(b_sent)
    a_sent = rearrange(
        join_kernel, (a_kept, a_back, in_hbm(b_sent)), 2 * QUARTERS, 2, cost=10_000_000_000
    )
    a_out = across(a_sent)
    mixed = finish_own(z, b_out, in_hbm(gate), in_hbm(product_b), skip)
    return finish_rest(
        z,
        a_out,
        b_back,
        in_hbm(gate),
        in_hbm(product_a),
        in_hbm(product_ao),
        in_hbm(product_b),
        skip,
        mixed,
    )


def solution(mesh):
    fine = Mesh(mesh.devices.reshape(4, 2, 4, 2, 4), ("x", "zh", "y", "core", "zl"))
    placed = (P(None, SEQ, "zl"), P(None, None, "zl"), P(None, SEQ + ("zl",)), P("zl"))
    return jax.shard_map(
        body, mesh=fine, in_specs=placed, out_specs=P(SEQ, "zl"), check_vma=False
    )
```

time: 183 us -> 155 us (0.85)
  waiting for transfers between devices: 72.6 us -> 58.6 us
  starting transfers between devices: 59 us -> 46.5 us
  other arithmetic: 4.27 us -> 0.07 us
    ppermute x4 -> x5, waiting for transfers between devices: 42.3 us -> 11.7 us  [swap_planes(): return lax.ppermute(x, 'zh', [(0, 1), (1, 0)])]
    all_to_all x4, waiting for transfers between devices: 27.3 us -> 46.8 us  [across(): return lax.all_to_all(x, PLANE, split_axis=0, concat_axis=0, tiled=True)]
    all_to_all x4, starting transfers between devices: 33.9 us -> 25.5 us  [across(): return lax.all_to_all(x, PLANE, split_axis=0, concat_axis=0, tiled=True)]
    all_to_all x1 -> x0, starting transfers between devices: 8.19 us -> none  [body(): lax.all_to_all(pieces, ('zh', 'zl'), split_axis=0, concat_axis=0, tiled=T...]
    ppermute x0 -> x3, starting transfers between devices: none -> 4.72 us  [body(): lax.ppermute(long_filter, 'zl', [(i, i ^ d) for i in range(4)])]
    concatenate x2 -> x1, other arithmetic: 3.12 us -> 0.07 us  [body(): place = jnp.concatenate([z, group])]
    pallas_call x9 -> x14, Pallas kernels: 40.5 us -> 41.7 us  [the longest x2 15.2 us: convolve(): pl.pallas_call(functools.partial(conv_kernel, layout, len(sources), len(o...]
    ppermute x4 -> x5, starting transfers between devices: 12.3 us -> 11.7 us  [swap_planes(): return lax.ppermute(x, 'zh', [(0, 1), (1, 0)])]
  transfers between devices with their start and end apart: 10 -> 13, of which waited for: 6 -> 6; matrix products, arithmetic and copies ran while one was open for 0% -> 0% of each run, Pallas kernels for 14% -> 24%
where the time goes in v2:
time: 155 us; the launch traced here: 152 us
  waiting for transfers between devices  58.6 us (38%)
  starting transfers between devices  46.5 us (30%)
  Pallas kernels  41.7 us (27%)
  local copies, waits for them, and re-layouts  5.14 us (3%)
    all_to_all x4, waiting for transfers between devices, across(): return lax.all_to_all(x, PLANE, split_axis=0, concat_axis=0, tiled=True)  46.8 us
    all_to_all x4, starting transfers between devices, across(): return lax.all_to_all(x, PLANE, split_axis=0, concat_axis=0, tiled=True)  25.5 us
    pallas_call x2, Pallas kernels, convolve(): pl.pallas_call(functools.partial(conv_kernel, layout, len(sources), len(o...  15.2 us
    ppermute x5, waiting for transfers between devices, swap_planes(): return lax.ppermute(x, 'zh', [(0, 1), (1, 0)])  11.7 us
    ppermute x5, starting transfers between devices, swap_planes(): return lax.ppermute(x, 'zh', [(0, 1), (1, 0)])  11.7 us
    pallas_call x4, Pallas kernels, from_streams(): pl.pallas_call(kernel, in_specs=[pl.BlockSpec(memory_space=pltpu.SMEM), p...  11 us
    pallas_call x4, Pallas kernels, rearrange(): pl.pallas_call(kernel, in_specs=in_specs, out_specs=anywhere, out_shape=j...  8.52 us
    ppermute x3, starting transfers between devices, body(): lax.ppermute(long_filter, 'zl', [(i, i ^ d) for i in range(4)])  4.72 us
  transfers between devices with their start and end apart: 13, of which 6 were waited for; matrix products, arithmetic and copies ran while one was open for 0% of the time, Pallas kernels for 24%

profile of v2, /device:TPU:1, one launch (start us, length us, event | category | flops | bytes accessed | tf_op | source)
XLA Modules:
  0.0 152.4 jit_solution(10388527851590458682)
XLA Ops:
  0.9 4.6 %collective-permute-start = (f32[3,8,1024]{2,1,0:T(8,128)S(1)}, f32[3,8,1024]{2,1,0:T(8,128)S(1)}, u32[]{:S(2)}, u32[]{:S(2)}) collective-permute-start(f32[3,8,1024]{2,1,0:T(8,128)S(1)} %slice.3), channel_id=1, source_target_pairs={{0,4},{4,8},{8,12},{12,16},{16,20},{20,24},{24,28},{28,32},{32,36}... | collective-permute-start | bytes 294920 | tf_op jit(solution)/shard_map/ppermute | solution.py:713
  5.5 3.1 %collective-permute-start.3 = (f32[4,128]{1,0:T(4,128)}, f32[4,128]{1,0:T(4,128)}, u32[]{:S(2)}, u32[]{:S(2)}) collective-permute-start(f32[4,128]{1,0:T(4,128)} %refs_0_.1), channel_id=1, source_target_pairs={{0,2},{1,3},{2,0},{3,1},{4,6},{5,7},{6,4},{7,5},{8,10},{9,11},{10,... | collective-permute-start | bytes 6152 | tf_op jit(solution)/shard_map/ppermute | solution.py:727
  10.2 2.7 %streams.4 = (f32[32,4,8,128]{3,2,1,0:T(8,128)}, f32[512,256]{1,0:T(8,128)S(1)}) custom-call(s32[1]{0:T(128)} %bitcast.z_ref, f32[3,8,1024]{2,1,0:T(8,128)S(1)} %collective-permute-done.halo_ref, f32[3,7,1024]{2,1,0:T(8,128)} %short_ref.7, f32[3,512,1024]{2,1,0:T(8,128)} %proj_ref.7), custom_call_target="tpu_custom_call" | custom-call | flops 1000000 | bytes 1000000 | tf_op jit(solution)/shard_map/streams/pallas_call | solution.py:384
  12.9 5.9 %collective-permute-start.1 = (f32[32,4,8,128]{3,2,1,0:T(8,128)}, f32[32,4,8,128]{3,2,1,0:T(8,128)}, u32[]{:S(2)}, u32[]{:S(2)}) collective-permute-start(f32[32,4,8,128]{3,2,1,0:T(8,128)} %get-tuple-element.17), channel_id=1, source_target_pairs={{0,32},{32,0},{1,33},{33,1},{2,34},{34,2},{3,35},{35,3},{4,36},{36... | collective-permute-start | bytes 1572872 | tf_op jit(solution)/shard_map/ppermute | solution.py:580
  18.8 3.5 %streams.5 = (f32[32,8,8,128]{3,2,1,0:T(8,128)}, f32[512,512]{1,0:T(8,128)S(1)}) custom-call(s32[1]{0:T(128)} %bitcast.z_ref, f32[3,8,1024]{2,1,0:T(8,128)S(1)} %collective-permute-done.halo_ref, f32[3,7,1024]{2,1,0:T(8,128)} %short_ref.7, f32[3,512,1024]{2,1,0:T(8,128)} %proj_ref.7, f32[512,256]{1,0:T(8,128)S(1)} %get-tuple-element.14.rest_0_.other_ref), custom_call_target="tpu_custom_call" | custom-call | flops 1000000 | bytes 1000000 | tf_op jit(solution)/shard_map/streams/pallas_call | solution.py:384
  22.4 11.1 %all-to-all-start = ((f32[32,8,8,128]{3,2,1,0:T(8,128)}), f32[32,8,8,128]{3,2,1,0:T(8,128)}, u32[]{:S(2)}, u32[]{:S(2)}) async-start(f32[32,8,8,128]{3,2,1,0:T(8,128)} %get-tuple-element.18), calls=%async_computation | async-start | bytes 2097152 | tf_op jit(solution)/shard_map/all_to_all | solution.py:584
  33.4 2.1 %streams.6 = (f32[32,4,8,128]{3,2,1,0:T(8,128)S(1)}, f32[512,256]{1,0:T(8,128)S(1)}) custom-call(s32[1]{0:T(128)} %bitcast.z_ref, f32[3,8,1024]{2,1,0:T(8,128)S(1)} %collective-permute-done.halo_ref, f32[3,7,1024]{2,1,0:T(8,128)} %short_ref.7, f32[3,512,1024]{2,1,0:T(8,128)} %proj_ref.7, f32[512,512]{1,0:T(8,128)S(1)} %get-tuple-element.15.rest_0_.product_ref.b_product_ref), custom_call_target="tpu_custom_call" | custom-call | flops 199999995904 | bytes 1000000 | tf_op jit(solution)/shard_map/streams/pallas_call | solution.py:384
  38.5 11.9 %all-to-all-done.both_ref.rest_1_ = f32[32,8,8,128]{3,2,1,0:T(8,128)} async-done(((f32[32,8,8,128]{3,2,1,0:T(8,128)}), f32[32,8,8,128]{3,2,1,0:T(8,128)}, u32[]{:S(2)}, u32[]{:S(2)}) %all-to-all-start) | async-done | bytes 1048608 | tf_op jit(solution)/shard_map/all_to_all | solution.py:584
  52.4 2.7 %rearrange.5 = f32[32,9,8,128]{3,2,1,0:T(8,128)} custom-call(s32[2]{0:T(128)S(1)} %pad_add_fusion.place_ref, f32[32,4,8,128]{3,2,1,0:T(8,128)} %copy-done.4, f32[32,4,8,128]{3,2,1,0:T(8,128)} %collective-permute-done.1.after_ref.from_ref.rest_0_, f32[16,128]{1,0:T(8,128)S(1)} %copy-done.5, f32[16,128]{1,0:T(8,128)S(1)} %collective-permute-done.5.there_ref, ...), custom_call_target="tpu_custom_call" | custom-call | flops 10000000000 | bytes 1000 | tf_op jit(solution)/shard_map/rearrange/pallas_call | solution.py:665
  55.1 4.6 %all-to-all-start.1 = ((f32[32,9,8,128]{3,2,1,0:T(8,128)}), f32[32,9,8,128]{3,2,1,0:T(8,128)}, u32[]{:S(2)}, u32[]{:S(2)}) async-start(f32[32,9,8,128]{3,2,1,0:T(8,128)} %rearrange.5), calls=%async_computation.1 | async-start | bytes 2359296 | tf_op jit(solution)/shard_map/all_to_all | solution.py:584
  59.7 2.7 %streams.7.refs_6_.gate_ref = f32[512,1024]{1,0:T(8,128)S(1)} custom-call(s32[1]{0:T(128)} %bitcast.z_ref, f32[3,8,1024]{2,1,0:T(8,128)S(1)} %collective-permute-done.halo_ref, f32[3,7,1024]{2,1,0:T(8,128)} %short_ref.7, f32[3,512,1024]{2,1,0:T(8,128)} %proj_ref.7, f32[32,4,8,128]{3,2,1,0:T(8,128)} %collective-permute-done.1.after_ref.from_ref.rest_0_, ...), custom_call_target="tpu_custom_call" | custom-call | flops 199999995904 | bytes 1000000 | tf_op jit(solution)/shard_map/streams/pallas_call | solution.py:384
  62.4 15.6 %all-to-all-done.1 = f32[32,9,8,128]{3,2,1,0:T(8,128)} async-done(((f32[32,9,8,128]{3,2,1,0:T(8,128)}), f32[32,9,8,128]{3,2,1,0:T(8,128)}, u32[]{:S(2)}, u32[]{:S(2)}) %all-to-all-start.1) | async-done | bytes 1179680 | tf_op jit(solution)/shard_map/all_to_all | solution.py:584
  78.0 7.3 %convolve.2 = (f32[1024,128]{1,0:T(8,128)S(1)}, f32[1024,128]{1,0:T(8,128)S(1)}, f32[256,256]{1,0:T(8,128)S(1)}) custom-call(s32[1]{0:T(128)} %bitcast.z_ref, f32[2304,128]{1,0:T(8,128)} %bitcast.2.refs_0_, bf16[512,512]{1,0:T(8,128)(2,1)} %constant.20.clone.refs_1_.refs_3_, bf16[256,1024]{1,0:T(8,128)(2,1)} %constant.21.clone.refs_2_.refs_4_, ...), custom_call_target="tpu_custom_call" | custom-call | flops 10000000 | bytes 1000000 | tf_op jit(solution)/shard_map/convolve/pallas_call | solution.py:556
  86.2 5.6 %collective-permute-start.6 = (f32[32,4,8,128]{3,2,1,0:T(8,128)S(1)}, f32[32,4,8,128]{3,2,1,0:T(8,128)S(1)}, u32[]{:S(2)}, u32[]{:S(2)}) collective-permute-start(f32[32,4,8,128]{3,2,1,0:T(8,128)S(1)} %bitcast.12), channel_id=1, source_target_pairs={{0,32},{32,0},{1,33},{33,1},{2,34},{34,2},{3,35},{35,3},{4,36},{36... | collective-permute-start | bytes 1572872 | tf_op jit(solution)/shard_map/ppermute | solution.py:580
  91.8 7.9 %convolve.3 = f32[2048,128]{1,0:T(8,128)} custom-call(s32[1]{0:T(128)} %bitcast.z_ref, f32[2048,128]{1,0:T(8,128)} %bitcast.5.refs_0_, f32[1024,128]{1,0:T(8,128)} %bitcast.6.refs_1_, f32[256,256]{1,0:T(8,128)S(1)} %get-tuple-element.21.refs_2_, bf16[512,512]{1,0:T(8,128)(2,1)} %constant.20.clone.refs_1_.refs_3_, ...), custom_call_target="tpu_custom_call" | custom-call | flops 10000000 | bytes 1000000 | tf_op jit(solution)/shard_map/convolve/pallas_call | solution.py:556
  99.7 4.8 %all-to-all-start.2 = ((f32[32,8,8,128]{3,2,1,0:T(8,128)}), f32[32,8,8,128]{3,2,1,0:T(8,128)}, u32[]{:S(2)}, u32[]{:S(2)}) async-start(f32[32,8,8,128]{3,2,1,0:T(8,128)} %bitcast.7), calls=%async_computation.2 | async-start | bytes 2097152 | tf_op jit(solution)/shard_map/all_to_all | solution.py:584
  104.5 2.0 %collective-permute-done.6.after_ref.from_ref = f32[32,4,8,128]{3,2,1,0:T(8,128)S(1)} collective-permute-done((f32[32,4,8,128]{3,2,1,0:T(8,128)S(1)}, f32[32,4,8,128]{3,2,1,0:T(8,128)S(1)}, u32[]{:S(2)}, u32[]{:S(2)}) %collective-permute-start.6) | collective-permute-done | bytes 524320 | tf_op jit(solution)/shard_map/ppermute | solution.py:580
  107.2 14.3 %all-to-all-done.2.both_ref.long_ref = f32[32,8,8,128]{3,2,1,0:T(8,128)} async-done(((f32[32,8,8,128]{3,2,1,0:T(8,128)}), f32[32,8,8,128]{3,2,1,0:T(8,128)}, u32[]{:S(2)}, u32[]{:S(2)}) %all-to-all-start.2) | async-done | bytes 1048608 | tf_op jit(solution)/shard_map/all_to_all | solution.py:584
  124.5 2.1 %rearrange.7 = f32[32,8,8,128]{3,2,1,0:T(8,128)} custom-call(f32[32,4,8,128]{3,2,1,0:T(8,128)} %bitcast.11, f32[32,4,8,128]{3,2,1,0:T(8,128)S(1)} %copy-done.9, f32[32,4,8,128]{3,2,1,0:T(8,128)} %rearrange.6.after_ref), custom_call_target="tpu_custom_call" | custom-call | flops 10000000000 | bytes 1000 | tf_op jit(solution)/shard_map/rearrange/pallas_call | solution.py:665
  126.7 5.1 %all-to-all-start.3 = ((f32[32,8,8,128]{3,2,1,0:T(8,128)}), f32[32,8,8,128]{3,2,1,0:T(8,128)}, u32[]{:S(2)}, u32[]{:S(2)}) async-start(f32[32,8,8,128]{3,2,1,0:T(8,128)} %rearrange.7), calls=%async_computation.3 | async-start | bytes 2097152 | tf_op jit(solution)/shard_map/all_to_all | solution.py:584
  131.7 2.2 %finish.2.whole_ref = f32[512,1024]{1,0:T(8,128)} custom-call(s32[1]{0:T(128)} %bitcast.z_ref, f32[32,8,8,128]{3,2,1,0:T(8,128)} %all-to-all-done.2.both_ref.long_ref, f32[512,1024]{1,0:T(8,128)} %copy-done, f32[512,512]{1,0:T(8,128)} %copy-done.2, f32[1,1024]{1,0:T(1,128)S(1)} %bitcast.9), custom_call_target="tpu_custom_call" | custom-call | flops 199999995904 | bytes 1000000 | tf_op jit(solution)/shard_map/finish/pallas_call | solution.py:442
  134.0 9.7 %collective-permute-done.8.b_ref = f32[32,4,8,128]{3,2,1,0:T(8,128)} collective-permute-done((f32[32,4,8,128]{3,2,1,0:T(8,128)}, f32[32,4,8,128]{3,2,1,0:T(8,128)}, u32[]{:S(2)}, u32[]{:S(2)}) %collective-permute-start.8) | collective-permute-done | bytes 524320 | tf_op jit(solution)/shard_map/ppermute | solution.py:580
  143.7 5.1 %all-to-all-done.3.a_ref = f32[32,8,8,128]{3,2,1,0:T(8,128)} async-done(((f32[32,8,8,128]{3,2,1,0:T(8,128)}), f32[32,8,8,128]{3,2,1,0:T(8,128)}, u32[]{:S(2)}, u32[]{:S(2)}) %all-to-all-start.3) | async-done | bytes 1048608 | tf_op jit(solution)/shard_map/all_to_all | solution.py:584
  148.8 3.4 %finish.3 = f32[512,1024]{1,0:T(8,128)} custom-call(s32[1]{0:T(128)} %bitcast.z_ref, f32[32,8,8,128]{3,2,1,0:T(8,128)} %all-to-all-done.3.a_ref, f32[32,4,8,128]{3,2,1,0:T(8,128)} %collective-permute-done.8.b_ref, f32[512,1024]{1,0:T(8,128)} %copy-done, f32[512,256]{1,0:T(8,128)} %copy-done.3, f32[512,256]{1,0:T(8,128)} %copy-done.1, ...), custom_call_target="tpu_custom_call", output_to_operand_aliasing={{}: (8, {})} | custom-call | flops 1000000 | bytes 1000000 | tf_op jit(solution)/shard_map/finish/pallas_call | solution.py:518
  (38 shorter events, 12.1 us)
Async XLA Ops:
  0.9 9.3 %collective-permute-start = (f32[3,8,1024]{2,1,0:T(8,128)S(1)}, f32[3,8,1024]{2,1,0:T(8,128)S(1)}, u32[]{:S(2)}, u32[]{:S(2)}) collective-permute-start(f32[3,8,1024]{2,1,0:T(8,128)S(1)} %slice.3), channel_id=1, source_target_pairs={{0,4},{4,8},{8,12},{12,16},{16,20},{20,24},{24,28},{28,32},{32,36}... | collective-permute-start | bytes 294920 | tf_op jit(solution)/shard_map/ppermute | solution.py:713
  5.5 31.6 %collective-permute-start.3 = (f32[4,128]{1,0:T(4,128)}, f32[4,128]{1,0:T(4,128)}, u32[]{:S(2)}, u32[]{:S(2)}) collective-permute-start(f32[4,128]{1,0:T(4,128)} %refs_0_.1), channel_id=1, source_target_pairs={{0,2},{1,3},{2,0},{3,1},{4,6},{5,7},{6,4},{7,5},{8,10},{9,11},{10,... | collective-permute-start | bytes 6152 | tf_op jit(solution)/shard_map/ppermute | solution.py:727
  8.6 28.5 %collective-permute-start.2 = (f32[4,128]{1,0:T(4,128)}, f32[4,128]{1,0:T(4,128)}, u32[]{:S(2)}, u32[]{:S(2)}) collective-permute-start(f32[4,128]{1,0:T(4,128)} %refs_0_.1), channel_id=1, source_target_pairs={{0,1},{1,0},{2,3},{3,2},{4,5},{5,4},{6,7},{7,6},{8,9},{9,8},{10,11... | collective-permute-start | bytes 6152 | tf_op jit(solution)/shard_map/ppermute | solution.py:727
  10.2 26.9 %collective-permute-start.4 = (f32[4,128]{1,0:T(4,128)}, f32[4,128]{1,0:T(4,128)}, u32[]{:S(2)}, u32[]{:S(2)}) collective-permute-start(f32[4,128]{1,0:T(4,128)} %refs_0_.1), channel_id=1, source_target_pairs={{0,3},{1,2},{2,1},{3,0},{4,7},{5,6},{6,5},{7,4},{8,11},{9,10},{10,... | collective-permute-start | bytes 6152 | tf_op jit(solution)/shard_map/ppermute | solution.py:727
  12.9 9.4 %copy-start.1 = (f32[512,256]{1,0:T(8,128)}, f32[512,256]{1,0:T(8,128)S(1)}, u32[]{:S(2)}) copy-start(f32[512,256]{1,0:T(8,128)S(1)} %get-tuple-element.14.rest_0_.other_ref) | copy-start | bytes 1572868
  12.9 25.5 %collective-permute-start.1 = (f32[32,4,8,128]{3,2,1,0:T(8,128)}, f32[32,4,8,128]{3,2,1,0:T(8,128)}, u32[]{:S(2)}, u32[]{:S(2)}) collective-permute-start(f32[32,4,8,128]{3,2,1,0:T(8,128)} %get-tuple-element.17), channel_id=1, source_target_pairs={{0,32},{32,0},{1,33},{33,1},{2,34},{34,2},{3,35},{35,3},{4,36},{36... | collective-permute-start | bytes 1572872 | tf_op jit(solution)/shard_map/ppermute | solution.py:580
  22.3 13.2 %copy-start.2 = (f32[512,512]{1,0:T(8,128)}, f32[512,512]{1,0:T(8,128)S(1)}, u32[]{:S(2)}) copy-start(f32[512,512]{1,0:T(8,128)S(1)} %get-tuple-element.15.rest_0_.product_ref.b_product_ref) | copy-start | bytes 3145732
  22.4 28.0 %all-to-all-start = ((f32[32,8,8,128]{3,2,1,0:T(8,128)}), f32[32,8,8,128]{3,2,1,0:T(8,128)}, u32[]{:S(2)}, u32[]{:S(2)}) async-start(f32[32,8,8,128]{3,2,1,0:T(8,128)} %get-tuple-element.18), calls=%async_computation | async-start | bytes 2097152 | tf_op jit(solution)/shard_map/all_to_all | solution.py:584
  35.5 0.8 copy-start.3
  36.3 0.8 copy-start.4
  38.4 14.0 %copy-start.5 = (f32[16,128]{1,0:T(8,128)S(1)}, f32[16,128]{1,0:T(8,128)}, u32[]{:S(2)}) copy-start(f32[16,128]{1,0:T(8,128)} %later.1.here_ref) | copy-start | bytes 24580
  38.4 14.0 %collective-permute-start.5 = (f32[16,128]{1,0:T(8,128)}, f32[16,128]{1,0:T(8,128)S(1)}, u32[]{:S(2)}, u32[]{:S(2)}) collective-permute-start(f32[16,128]{1,0:T(8,128)} %later.1.here_ref), channel_id=1, source_target_pairs={{0,32},{32,0},{1,33},{33,1},{2,34},{34,2},{3,35},{35,3},{4,36},{36... | collective-permute-start | bytes 24584 | tf_op jit(solution)/shard_map/ppermute | solution.py:580
  52.3 39.5 %collective-permute-start.7 = (f32[32,4,8,128]{3,2,1,0:T(8,128)}, f32[32,4,8,128]{3,2,1,0:T(8,128)}, u32[]{:S(2)}, u32[]{:S(2)}) collective-permute-start(f32[32,4,8,128]{3,2,1,0:T(8,128)} %rearrange.4.after_ref), channel_id=1, source_target_pairs={{0,32},{32,0},{1,33},{33,1},{2,34},{34,2},{3,35},{35,3},{4,36},{36... | collective-permute-start | bytes 1572872 | tf_op jit(solution)/shard_map/ppermute | solution.py:580
  55.1 23.0 %all-to-all-start.1 = ((f32[32,9,8,128]{3,2,1,0:T(8,128)}), f32[32,9,8,128]{3,2,1,0:T(8,128)}, u32[]{:S(2)}, u32[]{:S(2)}) async-start(f32[32,9,8,128]{3,2,1,0:T(8,128)} %rearrange.5), calls=%async_computation.1 | async-start | bytes 2359296 | tf_op jit(solution)/shard_map/all_to_all | solution.py:584
  62.4 23.0 %copy-start = (f32[512,1024]{1,0:T(8,128)}, f32[512,1024]{1,0:T(8,128)S(1)}, u32[]{:S(2)}) copy-start(f32[512,1024]{1,0:T(8,128)S(1)} %streams.7.refs_6_.gate_ref) | copy-start | bytes 6291460
  85.4 0.8 copy-start.7
  86.2 20.2 %collective-permute-start.6 = (f32[32,4,8,128]{3,2,1,0:T(8,128)S(1)}, f32[32,4,8,128]{3,2,1,0:T(8,128)S(1)}, u32[]{:S(2)}, u32[]{:S(2)}) collective-permute-start(f32[32,4,8,128]{3,2,1,0:T(8,128)S(1)} %bitcast.12), channel_id=1, source_target_pairs={{0,32},{32,0},{1,33},{33,1},{2,34},{34,2},{3,35},{35,3},{4,36},{36... | collective-permute-start | bytes 1572872 | tf_op jit(solution)/shard_map/ppermute | solution.py:580
  99.7 21.8 %all-to-all-start.2 = ((f32[32,8,8,128]{3,2,1,0:T(8,128)}), f32[32,8,8,128]{3,2,1,0:T(8,128)}, u32[]{:S(2)}, u32[]{:S(2)}) async-start(f32[32,8,8,128]{3,2,1,0:T(8,128)} %bitcast.7), calls=%async_computation.2 | async-start | bytes 2097152 | tf_op jit(solution)/shard_map/all_to_all | solution.py:584
  106.4 0.8 copy-start.8
  123.4 20.4 %collective-permute-start.8 = (f32[32,4,8,128]{3,2,1,0:T(8,128)}, f32[32,4,8,128]{3,2,1,0:T(8,128)}, u32[]{:S(2)}, u32[]{:S(2)}) collective-permute-start(f32[32,4,8,128]{3,2,1,0:T(8,128)} %rearrange.6.after_ref), channel_id=1, source_target_pairs={{0,32},{32,0},{1,33},{33,1},{2,34},{34,2},{3,35},{35,3},{4,36},{36... | collective-permute-start | bytes 1572872 | tf_op jit(solution)/shard_map/ppermute | solution.py:580
  123.5 1.0 copy-start.9
  126.7 5.1 %copy-start.6 = (f32[1024]{0:T(1024)S(1)}, f32[1024]{0:T(1024)}, u32[]{:S(2)}) copy-start(f32[1024]{0:T(1024)} %param.12) | copy-start | bytes 12292
  126.7 22.1 %all-to-all-start.3 = ((f32[32,8,8,128]{3,2,1,0:T(8,128)}), f32[32,8,8,128]{3,2,1,0:T(8,128)}, u32[]{:S(2)}, u32[]{:S(2)}) async-start(f32[32,8,8,128]{3,2,1,0:T(8,128)} %rearrange.7), calls=%async_computation.3 | async-start | bytes 2097152 | tf_op jit(solution)/shard_map/all_to_all | solution.py:584

commit v3 on v2

--- a/solution.py
+++ b/solution.py
@@ -24,6 +24,7 @@
 LENGTH = 32768
 VMEM_BYTES = 16 << 20
 CONV_BYTES = 40 << 20
+WHOLE_BYTES = 40 << 20
 SLOW = 200_000
 ORDER = 256
 
@@ -168,7 +169,6 @@
     first_ref, last_ref, onward_ref, back_ref, bend_ref = held[sources:inputs]
     out_refs = held[inputs:]
     low_plane = z_ref[0] == 0
-    wide = 2 * BLOCK if outputs == 1 else BLOCK
 
     for k in range(sources):
         wait_all(arrivals[k])
@@ -206,11 +206,8 @@
             row = q * PIECE + at
             rows_own = own[q * PEERS : (q + 1) * PEERS]
             rows_other = other[q * PEERS : (q + 1) * PEERS]
-            out_refs[0][pl.ds(row, PEERS, stride=wide), :] = rows_own
-            if outputs == 1:
-                out_refs[0][pl.ds(BLOCK + row, PEERS, stride=2 * BLOCK), :] = rows_other
-            else:
-                out_refs[1][pl.ds(row, PEERS, stride=BLOCK), :] = rows_other
+            out_refs[0][pl.ds(row, PEERS, stride=BLOCK), :] = rows_own
+            out_refs[1][pl.ds(row, PEERS, stride=BLOCK), :] = rows_other
 
     def load(channels):
         high, low = halves(jnp.concatenate([gather(at) for at in channels], axis=1))
@@ -276,7 +273,7 @@
             elif stage == len(stages):
                 for at, channel in enumerate(channels):
                     store(channel, state[batch][:, at * LANES : (at + 1) * LANES])
-    for k in range(min(outputs, 2)):
+    for k in (1, 0):
         leaving = leaving + copies_of(pieces_of(out_refs[k], results[k], CUTS), out_sems.at[k])
     wait_all(leaving)
 
@@ -341,43 +338,22 @@
     wait_all(leaving)
 
 
-def gate_kernel(z_ref, halo_ref, short_ref, proj_ref, *rest):
+def gate_kernel(chunk, z_ref, halo_ref, short_ref, proj_ref, *rest):
     gate_ref, buffer_ref, halo_held, taps_held, sems, out_sems, flat_ref = rest[-7:]
     step = 64
-    columns = [i * LANES for i in range(8)]
+    columns = [(chunk * 4 + i) * LANES for i in range(4)]
     blocks = fetch(
         proj_ref, halo_ref, short_ref, buffer_ref, halo_held, taps_held, sems, (0, 1), columns
     )
     leaving = []
     for i, copy in enumerate(blocks):
         copy.wait()
-        taps = taps_held[0, :, i * LANES : (i + 1) * LANES]
+        taps = taps_held[0, :, columns[i] : columns[i] + LANES]
         for at in range(0, ROWS, step):
             flat_ref[i, at : at + step, :] = short_sum(taps, buffer_ref.at[i, 0], at, step)
         pairs = [(flat_ref.at[i], gate_ref.at[:, pl.ds(i * LANES, LANES)])]
         leaving = leaving + copies_of(pairs, out_sems.at[i])
     wait_all(leaving)
-
-
-def final_kernel(z_ref, long_ref, gate_ref, product_ref, skip_ref, *rest):
-    out_ref = rest[-1]
-    skip = skip_ref[0:1, :]
-    for start in range(0, ROWS, LANES):
-        rows = slice(start, start + LANES)
-        turned = long_ref[:, start // LANES].reshape(LANES, LANES).T
-        out_ref[rows, :] = gate_ref[rows, :] * (turned + skip * product_ref[rows, :])
-
-
-def columns_of(chunk, slots):
-    def column(i, z_ref):
-        plane = z_ref[0]
-        if slots == (1,):
-            plane = 1 - plane
-        elif len(slots) == 2:
-            plane = jnp.where(i // 2 == 0, plane, 1 - plane)
-        return plane * 2 + i % 2 + chunk * 4
-
-    return column
 
 
 def from_streams(kernel, streams, blocks, extra, out_shape, weight, z, projected, halo, short_filter, after):
@@ -400,7 +376,7 @@
             pltpu.SemaphoreType.DMA((blocks, 2)),
         ]
         + extra,
-        compiler_params=pltpu.CompilerParams(vmem_limit_bytes=VMEM_BYTES),
+        compiler_params=pltpu.CompilerParams(vmem_limit_bytes=WHOLE_BYTES),
         cost_estimate=pl.CostEstimate(
             flops=weight * 1_000_000, bytes_accessed=1_000_000, transcendentals=0
         ),
@@ -408,16 +384,15 @@
     )(z, halo, short_filter, projected, *after)
 
 
-def features_of(z, chunk, slots, projected, halo, short_filter, after=(), weight=1):
-    count = len(slots)
-    blocks = 2 * count
+def features_of(z, parts, projected, halo, short_filter, after=(), weight=1):
+    blocks = 2 * len(parts)
 
     def columns_of_z(plane):
-        planes = [plane if slot == 0 else 1 - plane for slot in slots for _ in range(2)]
-        return [(chunk * 4 + planes[i] * 2 + i % 2) * LANES for i in range(blocks)]
+        firsts = [chunk * 4 + (1 - plane if slot else plane) * 2 for chunk, slot in parts]
+        return [(firsts[i // 2] + i % 2) * LANES for i in range(blocks)]
 
     out_shape = [
-        jax.ShapeDtypeStruct((PEERS, count * QUARTERS, PIECE, LANES), f32),
+        jax.ShapeDtypeStruct((PEERS, len(parts) * QUARTERS, PIECE, LANES), f32),
         jax.ShapeDtypeStruct((ROWS, blocks * LANES), f32),
     ]
     kernel = functools.partial(feature_kernel, columns_of_z)
@@ -430,47 +405,25 @@
     )
 
 
-def gates_of(z, projected, halo, short_filter, after):
-    out_shape = [jax.ShapeDtypeStruct((ROWS, 8 * LANES), f32)]
+def gates_of(z, chunk, projected, halo, short_filter, after):
+    out_shape = [jax.ShapeDtypeStruct((ROWS, 4 * LANES), f32)]
+    kernel = functools.partial(gate_kernel, chunk)
+    extra = [pltpu.VMEM((4, ROWS, LANES), f32)]
     return from_streams(
-        gate_kernel, 1, 8, [pltpu.VMEM((8, ROWS, LANES), f32)], out_shape, SLOW, z, projected, halo, short_filter, after
+        kernel, 1, 4, extra, out_shape, SLOW, z, projected, halo, short_filter, after
     )[0]
 
 
-def finish_own(z, b_out, gate, product_b, skip):
-    column = columns_of(1, (0,))
-    return pl.pallas_call(
-        final_kernel,
-        grid_spec=pltpu.PrefetchScalarGridSpec(
-            num_scalar_prefetch=1,
-            grid=(2,),
-            in_specs=[
-                pl.BlockSpec((LANES // PIECE, QUARTERS, PIECE, LANES), lambda i, z: (i, 0, 0, 0)),
-                pl.BlockSpec((ROWS, LANES), lambda i, z: (0, column(i, z))),
-                pl.BlockSpec((ROWS, LANES), lambda i, z: (0, i)),
-                pl.BlockSpec((1, LANES), lambda i, z: (0, column(i, z))),
-            ],
-            out_specs=pl.BlockSpec((ROWS, LANES), lambda i, z: (0, column(i, z))),
-        ),
-        out_shape=jax.ShapeDtypeStruct((ROWS, 8 * LANES), f32),
-        compiler_params=pltpu.CompilerParams(vmem_limit_bytes=VMEM_BYTES),
-        cost_estimate=pl.CostEstimate(
-            flops=SLOW * 1_000_000, bytes_accessed=1_000_000, transcendentals=0
-        ),
-        name="finish",
-    )(z, b_out, gate, product_b, skip)
-
-
-def finish_rest_kernel(
+def finish_kernel(
     z_ref,
-    a_ref,
+    out_part_ref,
     b_ref,
-    gate_ref,
+    gate_a_ref,
+    gate_b_ref,
     own_ref,
-    other_ref,
+    a_product_ref,
     b_product_ref,
     skip_ref,
-    whole_ref,
     out_ref,
     long_vmem,
     gate_vmem,
@@ -480,28 +433,33 @@
     out_sems,
 ):
     z = z_ref[0]
+    wide = 2 * LANES
     places = []
     arrivals = []
-    for i in range(3):
-        plane = z if i == 0 else 1 - z
-        column = pl.multiple_of(((0 if i < 2 else 4) + plane * 2) * LANES, 2 * LANES)
-        lanes = pl.ds(column, 2 * LANES)
+    for i in range(4):
+        plane = 1 - z if i % 2 else z
+        column = pl.multiple_of((i // 2 * 4 + plane * 2) * LANES, wide)
+        lanes = pl.ds(column, wide)
         places.append(lanes)
-        product = (own_ref, other_ref, b_product_ref)[i]
-        flat = pl.ds((2 if i == 2 else 0) * LANES, 2 * LANES)
+        half = pl.ds(pl.multiple_of(plane * wide, wide), wide)
+        if i % 2:
+            product = (a_product_ref, b_product_ref)[i // 2]
+        else:
+            product = own_ref.at[:, pl.ds(i // 2 * wide, wide)]
+        long = out_part_ref.at[:, pl.ds(QUARTERS * i, QUARTERS)] if i < 3 else b_ref
         pairs = [
-            (a_ref.at[:, pl.ds(QUARTERS * i, QUARTERS)] if i < 2 else b_ref, long_vmem.at[i]),
-            (gate_ref.at[:, lanes], gate_vmem.at[i]),
-            (product.at[:, flat], product_vmem.at[i]),
+            (long, long_vmem.at[i]),
+            ((gate_a_ref, gate_b_ref)[i // 2].at[:, half], gate_vmem.at[i]),
+            (product, product_vmem.at[i]),
         ]
         arrivals.append(copies_of(pairs, in_sems.at[i]))
     leaving = []
-    for i in range(3):
+    for i in range(4):
         wait_all(arrivals[i])
         skip = skip_ref[0:1, places[i]]
         for quarter in range(QUARTERS):
             rows = slice(quarter * LANES, (quarter + 1) * LANES)
-            turned = long_vmem[i, :, quarter].reshape(2 * LANES, LANES).T
+            turned = long_vmem[i, :, quarter].reshape(wide, LANES).T
             out_vmem[i, rows, :] = gate_vmem[i, rows, :] * (
                 turned + skip * product_vmem[i, rows, :]
             )
@@ -511,43 +469,36 @@
     wait_all(leaving)
 
 
-def finish_rest(z, a_out, b_back, gate, product_a, product_ao, product_b, skip, whole):
-    operands = [z, a_out, b_back, gate, product_a, product_ao, product_b, skip, whole]
+def finish(z, out_part, b_back, gate_a, gate_b, product_own, product_a, product_b, skip):
     anywhere = pl.BlockSpec(memory_space=pl.ANY)
-    flat = pltpu.VMEM((3, ROWS, 2 * LANES), f32)
+    flat = pltpu.VMEM((4, ROWS, 2 * LANES), f32)
     return pl.pallas_call(
-        finish_rest_kernel,
+        finish_kernel,
         in_specs=[pl.BlockSpec(memory_space=pltpu.SMEM)]
-        + [anywhere] * 6
-        + [pl.BlockSpec(memory_space=pltpu.VMEM), anywhere],
+        + [anywhere] * 7
+        + [pl.BlockSpec(memory_space=pltpu.VMEM)],
         out_specs=anywhere,
         out_shape=jax.ShapeDtypeStruct((ROWS, 8 * LANES), f32),
         scratch_shapes=[
-            pltpu.VMEM((3, PEERS, QUARTERS, PIECE, LANES), f32),
+            pltpu.VMEM((4, PEERS, QUARTERS, PIECE, LANES), f32),
             flat,
             flat,
             flat,
-            pltpu.SemaphoreType.DMA((3, 3)),
-            pltpu.SemaphoreType.DMA((3, 1)),
+            pltpu.SemaphoreType.DMA((4, 3)),
+            pltpu.SemaphoreType.DMA((4, 1)),
         ],
-        input_output_aliases={len(operands) - 1: 0},
         compiler_params=pltpu.CompilerParams(vmem_limit_bytes=CONV_BYTES),
         cost_estimate=pl.CostEstimate(
             flops=1_000_000, bytes_accessed=1_000_000, transcendentals=0
         ),
         name="finish",
-    )(*operands)
-
-
-def convolve(z, layout, sources, tables, joined, after=()):
-    if joined:
-        out_shape = [jax.ShapeDtypeStruct((2 * HALF, LANES), f32)]
-    else:
-        out_shape = [
-            jax.ShapeDtypeStruct((HALF, LANES), f32),
-            jax.ShapeDtypeStruct((HALF, LANES), f32),
-            jax.ShapeDtypeStruct((ORDER, 2 * LANES), f32),
-        ]
+    )(z, out_part, b_back, gate_a, gate_b, product_own, product_a, product_b, skip)
+
+
+def convolve(z, layout, sources, tables, after=()):
+    out_shape = [jax.ShapeDtypeStruct((HALF, LANES), f32)] * 2
+    if layout[-1] is not None:
+        out_shape = out_shape + [jax.ShapeDtypeStruct((ORDER, 2 * LANES), f32)]
     operands = list(sources) + [
         in_hbm(tables[name]) for name in ("first", "last", "onward", "back", "bend")
     ]
@@ -564,7 +515,7 @@
             pltpu.SemaphoreType.DMA((len(operands), CUTS)),
             pltpu.SemaphoreType.DMA((len(out_shape), CUTS)),
         ],
-        compiler_params=pltpu.CompilerParams(vmem_limit_bytes=CONV_BYTES),
+        compiler_params=pltpu.CompilerParams(vmem_limit_bytes=WHOLE_BYTES),
         cost_estimate=pl.CostEstimate(
             flops=10_000_000, bytes_accessed=1_000_000, transcendentals=0
         ),
@@ -606,7 +557,6 @@
     from_ref,
     here_ref,
     there_ref,
-    after_ref,
     out_ref,
     own_held,
     from_held,
@@ -617,8 +567,8 @@
     small_sems,
 ):
     pairs = [
-        (own_ref, out_ref.at[:, pl.ds(0, QUARTERS)]),
-        (from_ref, out_ref.at[:, pl.ds(QUARTERS, QUARTERS)]),
+        (own_ref, out_ref.at[:, pl.ds(0, 2 * QUARTERS)]),
+        (from_ref, out_ref.at[:, pl.ds(2 * QUARTERS, QUARTERS)]),
     ]
     small = [(here_ref, small_held.at[0]), (there_ref, small_held.at[1])]
     wait_all(copies_of(small, small_sems))
@@ -630,30 +580,21 @@
         there = small_held[1, pl.ds(row, 1), :]
         taps = jnp.where(z == zq // 4, here, there)
         taps_held[:, 0, zq : zq + 1, :] = jnp.broadcast_to(taps[None], (PEERS, 1, LANES))
-    into = out_ref.at[:, pl.ds(2 * QUARTERS, 1)]
+    into = out_ref.at[:, pl.ds(3 * QUARTERS, 1)]
     wait_all(leaving + copies_of([(taps_held, into)], small_sems))
 
 
-def join_kernel(own_ref, from_ref, after_ref, out_ref, own_held, from_held, in_sems, out_sems):
+def join_kernel(a_ref, from_ref, b_ref, out_ref, a_held, from_held, b_held, in_sems, out_sems):
     pairs = [
-        (own_ref, out_ref.at[:, pl.ds(0, QUARTERS)]),
-        (from_ref, out_ref.at[:, pl.ds(QUARTERS, QUARTERS)]),
+        (ref, out_ref.at[:, pl.ds(QUARTERS * at, QUARTERS)])
+        for at, ref in enumerate((a_ref, from_ref, b_ref))
     ]
-    wait_all(relay(pairs, (own_held, from_held), in_sems, out_sems))
-
-
-def cut_kernel(both_ref, after_ref, out_ref, held, in_sems, out_sems):
-    pairs = [(both_ref.at[:, pl.ds(QUARTERS, QUARTERS)], out_ref)]
-    wait_all(relay(pairs, (held,), in_sems, out_sems))
-
-
-def token_kernel(after_ref, out_ref):
-    pass
-
-
-def rearrange(kernel, operands, groups, pieces, place=None, cost=1_000):
+    wait_all(relay(pairs, (a_held, from_held, b_held), in_sems, out_sems))
+
+
+def rearrange(kernel, operands, groups, pieces, place=None, cost=10_000_000_000):
     anywhere = pl.BlockSpec(memory_space=pl.ANY)
-    scratch = [pltpu.VMEM((PEERS, QUARTERS, PIECE, LANES), f32)] * pieces
+    scratch = [pltpu.VMEM(x.shape, f32) for x in operands[:pieces]]
     scratch = scratch + [pltpu.SemaphoreType.DMA((pieces, CUTS))] * 2
     in_specs = [anywhere] * len(operands)
     if place is not None:
@@ -674,20 +615,6 @@
     )(*operands)
 
 
-def token(after):
-    anywhere = pl.BlockSpec(memory_space=pl.ANY)
-    return pl.pallas_call(
-        token_kernel,
-        in_specs=[anywhere],
-        out_specs=anywhere,
-        out_shape=jax.ShapeDtypeStruct((8, LANES), f32),
-        cost_estimate=pl.CostEstimate(
-            flops=SLOW * 1_000_000, bytes_accessed=1_000, transcendentals=0
-        ),
-        name="token",
-    )(after)
-
-
 def later_kernel(*refs):
     for at in range(4):
         refs[-1][at * 4 : (at + 1) * 4] = refs[at][...]
@@ -717,70 +644,64 @@
     feature = functools.partial(
         features_of, projected=projected, halo=halo, short_filter=short_filter
     )
-    a_other, product_ao = feature(z, 0, (1,))
+    a_other, product_a = feature(z, ((0, 1),))
     a_from = swap_planes(a_other)
-    b_both, product_b = feature(z, 1, (0, 1), after=(product_ao,))
-    b_here = across(b_both)
-    a_own, product_a = feature(z, 0, (0,), after=(product_b,), weight=SLOW)
+    b_other, product_b = feature(z, ((1, 1),), after=(product_a,))
+    b_there = across(b_other)
+    own, product_own = feature(z, ((0, 0), (1, 0)), after=(product_b,), weight=SLOW)
 
     steps = [
         lax.ppermute(long_filter, "zl", [(i, i ^ d) for i in range(4)]) for d in range(1, 4)
     ]
-    taps_here = later_rows((long_filter, *steps), a_own)
+    taps_here = later_rows((long_filter, *steps), own)
     taps_there = swap_planes(taps_here)
     group = lax.axis_index("zl").astype(jnp.int32).reshape(1)
     place = jnp.concatenate([z, group])
 
-    b_sent = rearrange(cut_kernel, (in_hbm(b_here), a_from), QUARTERS, 1)
-    b_from = swap_planes(b_sent)
-    a_sent = rearrange(
+    b_from = swap_planes(b_there)
+    sent = rearrange(
         join_taps_kernel,
-        (in_hbm(a_own), a_from, taps_here, taps_there, in_hbm(b_sent)),
-        2 * QUARTERS + 1,
+        (in_hbm(own), a_from, taps_here, taps_there),
+        3 * QUARTERS + 1,
         2,
         place=place,
-        cost=10_000_000_000,
-    )
-    a_here = across(a_sent)
-    gate = gates_of(z, projected, halo, short_filter, (a_from, b_here))
-    wide = 2 * BLOCK + 8
+    )
+    here = across(sent).reshape(-1, LANES)
+    gate_a = gates_of(z, 0, projected, halo, short_filter, (a_from, b_there))
+    wide = 3 * BLOCK + 8
     conv_a_own, conv_a_other, spectrum = convolve(
+        z, (0, wide, 2 * BLOCK, wide, 3 * BLOCK), (in_hbm(here),), tables, (gate_a,)
+    )
+
+    pieces = (PEERS, QUARTERS, PIECE, LANES)
+    a_back = swap_planes(conv_a_other.reshape(pieces))
+    conv_b_own, conv_b_other = convolve(
         z,
-        (0, wide, BLOCK, wide, 2 * BLOCK),
-        (in_hbm(a_here.reshape(-1, LANES)),),
+        (BLOCK, wide, 0, BLOCK, None),
+        (in_hbm(here), b_from.reshape(HALF, LANES), spectrum),
         tables,
-        False,
-        (gate,),
-    )
-
-    a_back = swap_planes(conv_a_other.reshape(PEERS, QUARTERS, PIECE, LANES))
-    (conv_b,) = convolve(
+    )
+    b_out = across(conv_b_other.reshape(pieces))
+
+    b_back = swap_planes(b_out)
+    gate_b = gates_of(z, 1, projected, halo, short_filter, (a_back, b_out))
+    sent = rearrange(
+        join_kernel,
+        (in_hbm(conv_a_own.reshape(pieces)), a_back, in_hbm(conv_b_own.reshape(pieces))),
+        3 * QUARTERS,
+        3,
+    )
+    out_part = across(sent)
+    return finish(
         z,
-        (0, 2 * BLOCK, 0, BLOCK, None),
-        (in_hbm(b_here.reshape(2 * HALF, LANES)), b_from.reshape(HALF, LANES), spectrum),
-        tables,
-        True,
-    )
-    b_out = across(conv_b.reshape(PEERS, 2 * QUARTERS, PIECE, LANES))
-
-    a_kept = in_hbm(conv_a_own.reshape(PEERS, QUARTERS, PIECE, LANES))
-    b_sent = rearrange(cut_kernel, (in_hbm(b_out), in_hbm(token(a_back))), QUARTERS, 1)
-    b_back = swap_planes(b_sent)
-    a_sent = rearrange(
-        join_kernel, (a_kept, a_back, in_hbm(b_sent)), 2 * QUARTERS, 2, cost=10_000_000_000
-    )
-    a_out = across(a_sent)
-    mixed = finish_own(z, b_out, in_hbm(gate), in_hbm(product_b), skip)
-    return finish_rest(
-        z,
-        a_out,
+        out_part,
         b_back,
-        in_hbm(gate),
+        in_hbm(gate_a),
+        in_hbm(gate_b),
+        in_hbm(product_own),
         in_hbm(product_a),
-        in_hbm(product_ao),
         in_hbm(product_b),
         skip,
-        mixed,
     )
 
 

time: 155 us -> 153 us (0.987); the launches traced: 152 us -> 153 us
  blocking collectives: 0 us -> 16.1 us
  waiting for transfers between devices: 58.6 us -> 48.8 us
  Pallas kernels: 41.7 us -> 37.4 us
  starting transfers between devices: 46.5 us -> 44.6 us
    all_to_all x0 -> x1, blocking collectives: none -> 16.1 us  [across(): return lax.all_to_all(x, PLANE, split_axis=0, concat_axis=0, tiled=True)]
    all_to_all x4 -> x3, waiting for transfers between devices: 46.8 us -> 41.3 us  [across(): return lax.all_to_all(x, PLANE, split_axis=0, concat_axis=0, tiled=True)]
    ppermute x5, waiting for transfers between devices: 11.7 us -> 7.48 us  [swap_planes(): return lax.ppermute(x, 'zh', [(0, 1), (1, 0)])]
    pallas_call x4 -> x2, Pallas kernels: 8.52 us -> 5.24 us  [rearrange(): pl.pallas_call(kernel, in_specs=in_specs, out_specs=anywhere, out_shape=j...]
    all_to_all x4 -> x3, starting transfers between devices: 25.5 us -> 24 us  [across(): return lax.all_to_all(x, PLANE, split_axis=0, concat_axis=0, tiled=True)]
    pallas_call x3 -> x1, Pallas kernels: 5.66 us -> 4.15 us  [finish(): pl.pallas_call(finish_kernel, in_specs=[pl.BlockSpec(memory_space=pltpu.S...]
    pallas_call x4 -> x5, Pallas kernels: 11 us -> 12.2 us  [from_streams(): pl.pallas_call(kernel, in_specs=[pl.BlockSpec(memory_space=pltpu.SMEM), p...]
  transfers between devices with their start and end apart: 13 -> 12, of which waited for: 6 -> 5; matrix products, arithmetic and copies ran while one was open for 0% -> 0% of each run, Pallas kernels for 24% -> 22%
where the time goes in v3:
time: 153 us
  waiting for transfers between devices  48.8 us (32%)
  starting transfers between devices  44.6 us (29%)
  Pallas kernels  37.4 us (24%)
  blocking collectives  16.1 us (11%)
  local copies, waits for them, and re-layouts  5.36 us (4%)
    all_to_all x3, waiting for transfers between devices, across(): return lax.all_to_all(x, PLANE, split_axis=0, concat_axis=0, tiled=True)  41.3 us
    all_to_all x3, starting transfers between devices, across(): return lax.all_to_all(x, PLANE, split_axis=0, concat_axis=0, tiled=True)  24 us
    all_to_all x1, blocking collectives, across(): return lax.all_to_all(x, PLANE, split_axis=0, concat_axis=0, tiled=True)  16.1 us
    pallas_call x2, Pallas kernels, convolve(): pl.pallas_call(functools.partial(conv_kernel, layout, len(sources), len(o...  14.5 us
    pallas_call x5, Pallas kernels, from_streams(): pl.pallas_call(kernel, in_specs=[pl.BlockSpec(memory_space=pltpu.SMEM), p...  12.2 us
    ppermute x5, starting transfers between devices, swap_planes(): return lax.ppermute(x, 'zh', [(0, 1), (1, 0)])  11.3 us
    ppermute x5, waiting for transfers between devices, swap_planes(): return lax.ppermute(x, 'zh', [(0, 1), (1, 0)])  7.48 us
    pallas_call x2, Pallas kernels, rearrange(): pl.pallas_call(kernel, in_specs=in_specs, out_specs=anywhere, out_shape=j...  5.24 us
  transfers between devices with their start and end apart: 12, of which 5 were waited for; matrix products, arithmetic and copies ran while one was open for 0% of the time, Pallas kernels for 22%

profile of v3, /device:TPU:1, one launch (start us, length us, event | category | flops | bytes accessed | tf_op | source)
XLA Modules:
  0.0 152.6 jit_solution(4703563005719332695)
XLA Ops:
  0.9 4.6 %collective-permute-start = (f32[3,8,1024]{2,1,0:T(8,128)S(1)}, f32[3,8,1024]{2,1,0:T(8,128)S(1)}, u32[]{:S(2)}, u32[]{:S(2)}) collective-permute-start(f32[3,8,1024]{2,1,0:T(8,128)S(1)} %slice.3), channel_id=1, source_target_pairs={{0,4},{4,8},{8,12},{12,16},{16,20},{20,24},{24,28},{28,32},{32,36}... | collective-permute-start | bytes 294920 | tf_op jit(solution)/shard_map/ppermute | solution.py:640
  5.5 3.1 %collective-permute-start.3 = (f32[4,128]{1,0:T(4,128)}, f32[4,128]{1,0:T(4,128)}, u32[]{:S(2)}, u32[]{:S(2)}) collective-permute-start(f32[4,128]{1,0:T(4,128)} %refs_0_.1), channel_id=1, source_target_pairs={{0,2},{1,3},{2,0},{3,1},{4,6},{5,7},{6,4},{7,5},{8,10},{9,11},{10,... | collective-permute-start | bytes 6152 | tf_op jit(solution)/shard_map/ppermute | solution.py:654
  8.6 1.6 %collective-permute-start.2 = (f32[4,128]{1,0:T(4,128)}, f32[4,128]{1,0:T(4,128)}, u32[]{:S(2)}, u32[]{:S(2)}) collective-permute-start(f32[4,128]{1,0:T(4,128)} %refs_0_.1), channel_id=1, source_target_pairs={{0,1},{1,0},{2,3},{3,2},{4,5},{5,4},{6,7},{7,6},{8,9},{9,8},{10,11... | collective-permute-start | bytes 6152 | tf_op jit(solution)/shard_map/ppermute | solution.py:654
  10.2 2.7 %streams.5 = (f32[32,4,8,128]{3,2,1,0:T(8,128)}, f32[512,256]{1,0:T(8,128)S(1)}) custom-call(s32[1]{0:T(128)} %bitcast.z_ref, f32[3,8,1024]{2,1,0:T(8,128)S(1)} %collective-permute-done.halo_ref, f32[3,7,1024]{2,1,0:T(8,128)} %short_ref.9, f32[3,512,1024]{2,1,0:T(8,128)} %proj_ref.9), custom_call_target="tpu_custom_call" | custom-call | flops 1000000 | bytes 1000000 | tf_op jit(solution)/shard_map/streams/pallas_call | solution.py:360
  12.9 5.9 %collective-permute-start.1 = (f32[32,4,8,128]{3,2,1,0:T(8,128)}, f32[32,4,8,128]{3,2,1,0:T(8,128)}, u32[]{:S(2)}, u32[]{:S(2)}) collective-permute-start(f32[32,4,8,128]{3,2,1,0:T(8,128)} %get-tuple-element.19), channel_id=1, source_target_pairs={{0,32},{32,0},{1,33},{33,1},{2,34},{34,2},{3,35},{35,3},{4,36},{36... | collective-permute-start | bytes 1572872 | tf_op jit(solution)/shard_map/ppermute | solution.py:531
  18.8 2.7 %streams.6 = (f32[32,4,8,128]{3,2,1,0:T(8,128)}, f32[512,256]{1,0:T(8,128)S(1)}) custom-call(s32[1]{0:T(128)} %bitcast.z_ref, f32[3,8,1024]{2,1,0:T(8,128)S(1)} %collective-permute-done.halo_ref, f32[3,7,1024]{2,1,0:T(8,128)} %short_ref.9, f32[3,512,1024]{2,1,0:T(8,128)} %proj_ref.9, f32[512,256]{1,0:T(8,128)S(1)} %get-tuple-element.16.rest_0_.a_product_ref), custom_call_target="tpu_custom_call" | custom-call | flops 1000000 | bytes 1000000 | tf_op jit(solution)/shard_map/streams/pallas_call | solution.py:360
  21.5 11.1 %all-to-all-start.1 = ((f32[32,4,8,128]{3,2,1,0:T(8,128)}), f32[32,4,8,128]{3,2,1,0:T(8,128)}, u32[]{:S(2)}, u32[]{:S(2)}) async-start(f32[32,4,8,128]{3,2,1,0:T(8,128)} %get-tuple-element.20), calls=%async_computation.1 | async-start | bytes 1048576 | tf_op jit(solution)/shard_map/all_to_all | solution.py:535
  32.6 2.9 %streams.7 = (f32[32,8,8,128]{3,2,1,0:T(8,128)S(1)}, f32[512,512]{1,0:T(8,128)S(1)}) custom-call(s32[1]{0:T(128)} %bitcast.z_ref, f32[3,8,1024]{2,1,0:T(8,128)S(1)} %collective-permute-done.halo_ref, f32[3,7,1024]{2,1,0:T(8,128)} %short_ref.9, f32[3,512,1024]{2,1,0:T(8,128)} %proj_ref.9, f32[512,256]{1,0:T(8,128)S(1)} %get-tuple-element.17.rest_0_.b_product_ref), custom_call_target="tpu_custom_call" | custom-call | flops 199999995904 | bytes 1000000 | tf_op jit(solution)/shard_map/streams/pallas_call | solution.py:360
  38.9 5.3 %all-to-all-done.1.rest_1_ = f32[32,4,8,128]{3,2,1,0:T(8,128)} async-done(((f32[32,4,8,128]{3,2,1,0:T(8,128)}), f32[32,4,8,128]{3,2,1,0:T(8,128)}, u32[]{:S(2)}, u32[]{:S(2)}) %all-to-all-start.1) | async-done | bytes 524320 | tf_op jit(solution)/shard_map/all_to_all | solution.py:535
  44.3 1.4 collective-permute-done.5.there_ref
  46.5 3.0 %rearrange.2 = f32[32,13,8,128]{3,2,1,0:T(8,128)} custom-call(s32[2]{0:T(128)S(1)} %pad_add_fusion.place_ref, f32[32,8,8,128]{3,2,1,0:T(8,128)} %copy-done.2, f32[32,4,8,128]{3,2,1,0:T(8,128)} %collective-permute-done.1.from_ref.rest_0_, f32[16,128]{1,0:T(8,128)S(1)} %copy-done.6, f32[16,128]{1,0:T(8,128)S(1)} %collective-permute-done.5.there_ref), custom_call_target="tpu_custom_call" | custom-call | flops 10000000000 | bytes 1000 | tf_op jit(solution)/shard_map/rearrange/pallas_call | solution.py:606
  49.5 8.4 %all-to-all-start = ((f32[32,13,8,128]{3,2,1,0:T(8,128)}), f32[32,13,8,128]{3,2,1,0:T(8,128)}, u32[]{:S(2)}, u32[]{:S(2)}) async-start(f32[32,13,8,128]{3,2,1,0:T(8,128)} %rearrange.2), calls=%async_computation | async-start | bytes 3407872 | tf_op jit(solution)/shard_map/all_to_all | solution.py:535
  57.9 1.9 %streams.8.refs_6_.gate_a_ref = f32[512,512]{1,0:T(8,128)S(1)} custom-call(s32[1]{0:T(128)} %bitcast.z_ref, f32[3,8,1024]{2,1,0:T(8,128)S(1)} %collective-permute-done.halo_ref, f32[3,7,1024]{2,1,0:T(8,128)} %short_ref.9, f32[3,512,1024]{2,1,0:T(8,128)} %proj_ref.9, f32[32,4,8,128]{3,2,1,0:T(8,128)} %collective-permute-done.1.from_ref.rest_0_, ...), custom_call_target="tpu_custom_call" | custom-call | flops 199999995904 | bytes 1000000 | tf_op jit(solution)/shard_map/streams/pallas_call | solution.py:360
  59.9 22.2 %all-to-all-done = f32[32,13,8,128]{3,2,1,0:T(8,128)} async-done(((f32[32,13,8,128]{3,2,1,0:T(8,128)}), f32[32,13,8,128]{3,2,1,0:T(8,128)}, u32[]{:S(2)}, u32[]{:S(2)}) %all-to-all-start) | async-done | bytes 1703968 | tf_op jit(solution)/shard_map/all_to_all | solution.py:535
  82.1 7.5 %convolve.2 = (f32[1024,128]{1,0:T(8,128)S(1)}, f32[1024,128]{1,0:T(8,128)S(1)}, f32[256,256]{1,0:T(8,128)S(1)}) custom-call(s32[1]{0:T(128)} %bitcast.z_ref, f32[3328,128]{1,0:T(8,128)} %bitcast.2.refs_0_, bf16[512,512]{1,0:T(8,128)(2,1)} %constant.20.clone.refs_1_.refs_3_, bf16[256,1024]{1,0:T(8,128)(2,1)} %constant.21.clone.refs_2_.refs_4_, ...), custom_call_target="tpu_custom_call" | custom-call | flops 10000000 | bytes 1000000 | tf_op jit(solution)/shard_map/convolve/pallas_call | solution.py:507
  90.6 7.0 %convolve.3 = (f32[1024,128]{1,0:T(8,128)S(1)}, f32[1024,128]{1,0:T(8,128)S(1)}) custom-call(s32[1]{0:T(128)} %bitcast.z_ref, f32[3328,128]{1,0:T(8,128)} %bitcast.2.refs_0_, f32[1024,128]{1,0:T(8,128)} %bitcast.5.refs_1_, f32[256,256]{1,0:T(8,128)S(1)} %get-tuple-element.23.refs_2_, bf16[512,512]{1,0:T(8,128)(2,1)} %constant.20.clone.refs_1_.refs_3_, ...), custom_call_target="tpu_custom_call" | custom-call | flops 10000000 | bytes 1000000 | tf_op jit(solution)/shard_map/convolve/pallas_call | solution.py:507
  97.7 16.1 %all_to_all.20.rest_1_ = f32[32,4,8,128]{3,2,1,0:T(8,128)} all-to-all(f32[32,4,8,128]{3,2,1,0:T(8,128)S(1)} %bitcast.9), channel_id=1, replica_groups=mesh['x'=4,'zh'=2,'y'=4,'core'=2,'zl'=4] {'x','y','core'}, dimensions={0} | all-to-all | bytes 1048576 | tf_op jit(solution)/shard_map/all_to_all | solution.py:535
  113.7 5.1 %collective-permute-start.8 = (f32[32,4,8,128]{3,2,1,0:T(8,128)}, f32[32,4,8,128]{3,2,1,0:T(8,128)}, u32[]{:S(2)}, u32[]{:S(2)}) collective-permute-start(f32[32,4,8,128]{3,2,1,0:T(8,128)} %all_to_all.20.rest_1_), channel_id=1, source_target_pairs={{0,32},{32,0},{1,33},{33,1},{2,34},{34,2},{3,35},{35,3},{4,36},{36... | collective-permute-start | bytes 1572872 | tf_op jit(solution)/shard_map/ppermute | solution.py:531
  118.9 2.2 %rearrange.3 = f32[32,12,8,128]{3,2,1,0:T(8,128)} custom-call(f32[32,4,8,128]{3,2,1,0:T(8,128)} %bitcast.11, f32[32,4,8,128]{3,2,1,0:T(8,128)S(1)} %collective-permute-done.6.from_ref.rest_0_, f32[32,4,8,128]{3,2,1,0:T(8,128)} %bitcast.13), custom_call_target="tpu_custom_call" | custom-call | flops 10000000000 | bytes 1000 | tf_op jit(solution)/shard_map/rearrange/pallas_call | solution.py:606
  121.1 4.5 %all-to-all-start.2 = ((f32[32,12,8,128]{3,2,1,0:T(8,128)}), f32[32,12,8,128]{3,2,1,0:T(8,128)}, u32[]{:S(2)}, u32[]{:S(2)}) async-start(f32[32,12,8,128]{3,2,1,0:T(8,128)} %rearrange.3), calls=%async_computation.2 | async-start | bytes 3145728 | tf_op jit(solution)/shard_map/all_to_all | solution.py:535
  125.6 1.9 %streams.9.gate_b_ref = f32[512,512]{1,0:T(8,128)S(1)} custom-call(s32[1]{0:T(128)} %bitcast.z_ref, f32[3,8,1024]{2,1,0:T(8,128)S(1)} %collective-permute-done.halo_ref, f32[3,7,1024]{2,1,0:T(8,128)} %short_ref.9, f32[3,512,1024]{2,1,0:T(8,128)} %proj_ref.9, f32[32,4,8,128]{3,2,1,0:T(8,128)S(1)} %collective-permute-done.6.from_ref.rest_0_, ...), custom_call_target="tpu_custom_call" | custom-call | flops 199999995904 | bytes 1000000 | tf_op jit(solution)/shard_map/streams/pallas_call | solution.py:360
  128.5 6.0 %collective-permute-done.8.b_ref = f32[32,4,8,128]{3,2,1,0:T(8,128)} collective-permute-done((f32[32,4,8,128]{3,2,1,0:T(8,128)}, f32[32,4,8,128]{3,2,1,0:T(8,128)}, u32[]{:S(2)}, u32[]{:S(2)}) %collective-permute-start.8) | collective-permute-done | bytes 524320 | tf_op jit(solution)/shard_map/ppermute | solution.py:531
  134.6 13.7 %all-to-all-done.2.out_part_ref = f32[32,12,8,128]{3,2,1,0:T(8,128)} async-done(((f32[32,12,8,128]{3,2,1,0:T(8,128)}), f32[32,12,8,128]{3,2,1,0:T(8,128)}, u32[]{:S(2)}, u32[]{:S(2)}) %all-to-all-start.2) | async-done | bytes 1572896 | tf_op jit(solution)/shard_map/all_to_all | solution.py:535
  148.3 4.1 %finish.1 = f32[512,1024]{1,0:T(8,128)} custom-call(s32[1]{0:T(128)} %bitcast.z_ref, f32[32,12,8,128]{3,2,1,0:T(8,128)} %all-to-all-done.2.out_part_ref, f32[32,4,8,128]{3,2,1,0:T(8,128)} %collective-permute-done.8.b_ref, f32[512,512]{1,0:T(8,128)} %copy-done, f32[512,512]{1,0:T(8,128)} %copy-done.4, f32[512,512]{1,0:T(8,128)} %copy-done.3, ...), custom_call_target="tpu_custom_call" | custom-call | flops 1000000 | bytes 1000000 | tf_op jit(solution)/shard_map/finish/pallas_call | solution.py:475
  (34 shorter events, 7.1 us)
Async XLA Ops:
  0.9 9.3 %collective-permute-start = (f32[3,8,1024]{2,1,0:T(8,128)S(1)}, f32[3,8,1024]{2,1,0:T(8,128)S(1)}, u32[]{:S(2)}, u32[]{:S(2)}) collective-permute-start(f32[3,8,1024]{2,1,0:T(8,128)S(1)} %slice.3), channel_id=1, source_target_pairs={{0,4},{4,8},{8,12},{12,16},{16,20},{20,24},{24,28},{28,32},{32,36}... | collective-permute-start | bytes 294920 | tf_op jit(solution)/shard_map/ppermute | solution.py:640
  5.5 32.1 %collective-permute-start.3 = (f32[4,128]{1,0:T(4,128)}, f32[4,128]{1,0:T(4,128)}, u32[]{:S(2)}, u32[]{:S(2)}) collective-permute-start(f32[4,128]{1,0:T(4,128)} %refs_0_.1), channel_id=1, source_target_pairs={{0,2},{1,3},{2,0},{3,1},{4,6},{5,7},{6,4},{7,5},{8,10},{9,11},{10,... | collective-permute-start | bytes 6152 | tf_op jit(solution)/shard_map/ppermute | solution.py:654
  8.6 29.0 %collective-permute-start.2 = (f32[4,128]{1,0:T(4,128)}, f32[4,128]{1,0:T(4,128)}, u32[]{:S(2)}, u32[]{:S(2)}) collective-permute-start(f32[4,128]{1,0:T(4,128)} %refs_0_.1), channel_id=1, source_target_pairs={{0,1},{1,0},{2,3},{3,2},{4,5},{5,4},{6,7},{7,6},{8,9},{9,8},{10,11... | collective-permute-start | bytes 6152 | tf_op jit(solution)/shard_map/ppermute | solution.py:654
  10.2 27.4 %collective-permute-start.4 = (f32[4,128]{1,0:T(4,128)}, f32[4,128]{1,0:T(4,128)}, u32[]{:S(2)}, u32[]{:S(2)}) collective-permute-start(f32[4,128]{1,0:T(4,128)} %refs_0_.1), channel_id=1, source_target_pairs={{0,3},{1,2},{2,1},{3,0},{4,7},{5,6},{6,5},{7,4},{8,11},{9,10},{10,... | collective-permute-start | bytes 6152 | tf_op jit(solution)/shard_map/ppermute | solution.py:654
  12.9 8.6 %copy-start.1 = (f32[512,256]{1,0:T(8,128)}, f32[512,256]{1,0:T(8,128)S(1)}, u32[]{:S(2)}) copy-start(f32[512,256]{1,0:T(8,128)S(1)} %get-tuple-element.16.rest_0_.a_product_ref) | copy-start | bytes 1572868
  12.9 32.8 %collective-permute-start.1 = (f32[32,4,8,128]{3,2,1,0:T(8,128)}, f32[32,4,8,128]{3,2,1,0:T(8,128)}, u32[]{:S(2)}, u32[]{:S(2)}) collective-permute-start(f32[32,4,8,128]{3,2,1,0:T(8,128)} %get-tuple-element.19), channel_id=1, source_target_pairs={{0,32},{32,0},{1,33},{33,1},{2,34},{34,2},{3,35},{35,3},{4,36},{36... | collective-permute-start | bytes 1572872 | tf_op jit(solution)/shard_map/ppermute | solution.py:531
  21.5 14.0 %copy-start.5 = (f32[512,256]{1,0:T(8,128)}, f32[512,256]{1,0:T(8,128)S(1)}, u32[]{:S(2)}) copy-start(f32[512,256]{1,0:T(8,128)S(1)} %get-tuple-element.17.rest_0_.b_product_ref) | copy-start | bytes 1572868
  21.5 22.7 %all-to-all-start.1 = ((f32[32,4,8,128]{3,2,1,0:T(8,128)}), f32[32,4,8,128]{3,2,1,0:T(8,128)}, u32[]{:S(2)}, u32[]{:S(2)}) async-start(f32[32,4,8,128]{3,2,1,0:T(8,128)} %get-tuple-element.20), calls=%async_computation.1 | async-start | bytes 1048576 | tf_op jit(solution)/shard_map/all_to_all | solution.py:535
  35.6 1.0 copy-start.2
  36.6 1.0 copy-start.3
  38.9 6.9 %collective-permute-start.5 = (f32[16,128]{1,0:T(8,128)}, f32[16,128]{1,0:T(8,128)S(1)}, u32[]{:S(2)}, u32[]{:S(2)}) collective-permute-start(f32[16,128]{1,0:T(8,128)} %later.1.here_ref), channel_id=1, source_target_pairs={{0,32},{32,0},{1,33},{33,1},{2,34},{34,2},{3,35},{35,3},{4,36},{36... | collective-permute-start | bytes 24584 | tf_op jit(solution)/shard_map/ppermute | solution.py:531
  44.3 46.3 %collective-permute-start.7 = (f32[32,4,8,128]{3,2,1,0:T(8,128)}, f32[32,4,8,128]{3,2,1,0:T(8,128)}, u32[]{:S(2)}, u32[]{:S(2)}) collective-permute-start(f32[32,4,8,128]{3,2,1,0:T(8,128)} %all-to-all-done.1.rest_1_), channel_id=1, source_target_pairs={{0,32},{32,0},{1,33},{33,1},{2,34},{34,2},{3,35},{35,3},{4,36},{36... | collective-permute-start | bytes 1572872 | tf_op jit(solution)/shard_map/ppermute | solution.py:531
  45.8 0.7 copy-start.6
  49.5 32.5 %all-to-all-start = ((f32[32,13,8,128]{3,2,1,0:T(8,128)}), f32[32,13,8,128]{3,2,1,0:T(8,128)}, u32[]{:S(2)}, u32[]{:S(2)}) async-start(f32[32,13,8,128]{3,2,1,0:T(8,128)} %rearrange.2), calls=%async_computation | async-start | bytes 3407872 | tf_op jit(solution)/shard_map/all_to_all | solution.py:535
  59.8 29.7 %copy-start = (f32[512,512]{1,0:T(8,128)}, f32[512,512]{1,0:T(8,128)S(1)}, u32[]{:S(2)}) copy-start(f32[512,512]{1,0:T(8,128)S(1)} %streams.8.refs_6_.gate_a_ref) | copy-start | bytes 3145732
  89.6 0.8 copy-start.8
  90.4 28.5 %collective-permute-start.6 = (f32[32,4,8,128]{3,2,1,0:T(8,128)S(1)}, f32[32,4,8,128]{3,2,1,0:T(8,128)S(1)}, u32[]{:S(2)}, u32[]{:S(2)}) collective-permute-start(f32[32,4,8,128]{3,2,1,0:T(8,128)S(1)} %bitcast.12), channel_id=1, source_target_pairs={{0,32},{32,0},{1,33},{33,1},{2,34},{34,2},{3,35},{35,3},{4,36},{36... | collective-permute-start | bytes 1572872 | tf_op jit(solution)/shard_map/ppermute | solution.py:531
  97.7 21.2 %copy-start.9 = (f32[1024,128]{1,0:T(8,128)}, f32[1024,128]{1,0:T(8,128)S(1)}, u32[]{:S(2)}) copy-start(f32[1024,128]{1,0:T(8,128)S(1)} %get-tuple-element.24) | copy-start | bytes 1572868
  113.7 20.8 %collective-permute-start.8 = (f32[32,4,8,128]{3,2,1,0:T(8,128)}, f32[32,4,8,128]{3,2,1,0:T(8,128)}, u32[]{:S(2)}, u32[]{:S(2)}) collective-permute-start(f32[32,4,8,128]{3,2,1,0:T(8,128)} %all_to_all.20.rest_1_), channel_id=1, source_target_pairs={{0,32},{32,0},{1,33},{33,1},{2,34},{34,2},{3,35},{35,3},{4,36},{36... | collective-permute-start | bytes 1572872 | tf_op jit(solution)/shard_map/ppermute | solution.py:531
  121.1 27.2 %all-to-all-start.2 = ((f32[32,12,8,128]{3,2,1,0:T(8,128)}), f32[32,12,8,128]{3,2,1,0:T(8,128)}, u32[]{:S(2)}, u32[]{:S(2)}) async-start(f32[32,12,8,128]{3,2,1,0:T(8,128)} %rearrange.3), calls=%async_computation.2 | async-start | bytes 3145728 | tf_op jit(solution)/shard_map/all_to_all | solution.py:535
  125.6 22.7 %copy-start.7 = (f32[1024]{0:T(1024)S(1)}, f32[1024]{0:T(1024)}, u32[]{:S(2)}) copy-start(f32[1024]{0:T(1024)} %param.12) | copy-start | bytes 12292
  127.6 1.0 copy-start.4

commit v4 on v3

--- a/solution.py
+++ b/solution.py
@@ -426,15 +426,14 @@
     skip_ref,
     out_ref,
     long_vmem,
-    gate_vmem,
-    product_vmem,
+    own_vmem,
     out_vmem,
     in_sems,
     out_sems,
 ):
     z = z_ref[0]
     wide = 2 * LANES
-    places = []
+    places, products, gates = [], [], []
     arrivals = []
     for i in range(4):
         plane = 1 - z if i % 2 else z
@@ -443,15 +442,15 @@
         places.append(lanes)
         half = pl.ds(pl.multiple_of(plane * wide, wide), wide)
         if i % 2:
-            product = (a_product_ref, b_product_ref)[i // 2]
+            products.append((a_product_ref, slice(0, wide)) if i < 2 else (b_product_ref, slice(0, wide)))
         else:
-            product = own_ref.at[:, pl.ds(i // 2 * wide, wide)]
+            products.append((own_vmem.at[i // 2], slice(0, wide)))
+        gates.append(((gate_a_ref, gate_b_ref)[i // 2], half))
         long = out_part_ref.at[:, pl.ds(QUARTERS * i, QUARTERS)] if i < 3 else b_ref
-        pairs = [
-            (long, long_vmem.at[i]),
-            ((gate_a_ref, gate_b_ref)[i // 2].at[:, half], gate_vmem.at[i]),
-            (product, product_vmem.at[i]),
-        ]
+        pairs = [(long, long_vmem.at[i])]
+        if i % 2 == 0:
+            own = own_ref.at[:, pl.ds(i // 2 * wide, wide)]
+            pairs.append((own, own_vmem.at[i // 2]))
         arrivals.append(copies_of(pairs, in_sems.at[i]))
     leaving = []
     for i in range(4):
@@ -460,9 +459,9 @@
         for quarter in range(QUARTERS):
             rows = slice(quarter * LANES, (quarter + 1) * LANES)
             turned = long_vmem[i, :, quarter].reshape(wide, LANES).T
-            out_vmem[i, rows, :] = gate_vmem[i, rows, :] * (
-                turned + skip * product_vmem[i, rows, :]
-            )
+            gate, half = gates[i]
+            product, lanes = products[i]
+            out_vmem[i, rows, :] = gate[rows, half] * (turned + skip * product[rows, lanes])
         leaving = leaving + copies_of(
             [(out_vmem.at[i], out_ref.at[:, places[i]])], out_sems.at[i]
         )
@@ -475,16 +474,17 @@
     return pl.pallas_call(
         finish_kernel,
         in_specs=[pl.BlockSpec(memory_space=pltpu.SMEM)]
-        + [anywhere] * 7
-        + [pl.BlockSpec(memory_space=pltpu.VMEM)],
+        + [anywhere] * 2
+        + [pl.BlockSpec(memory_space=pltpu.VMEM)] * 2
+        + [anywhere]
+        + [pl.BlockSpec(memory_space=pltpu.VMEM)] * 3,
         out_specs=anywhere,
         out_shape=jax.ShapeDtypeStruct((ROWS, 8 * LANES), f32),
         scratch_shapes=[
             pltpu.VMEM((4, PEERS, QUARTERS, PIECE, LANES), f32),
+            pltpu.VMEM((2, ROWS, 2 * LANES), f32),
             flat,
-            flat,
-            flat,
-            pltpu.SemaphoreType.DMA((4, 3)),
+            pltpu.SemaphoreType.DMA((4, 2)),
             pltpu.SemaphoreType.DMA((4, 1)),
         ],
         compiler_params=pltpu.CompilerParams(vmem_limit_bytes=CONV_BYTES),
@@ -696,11 +696,11 @@
         z,
         out_part,
         b_back,
-        in_hbm(gate_a),
-        in_hbm(gate_b),
+        gate_a,
+        gate_b,
         in_hbm(product_own),
-        in_hbm(product_a),
-        in_hbm(product_b),
+        product_a,
+        product_b,
         skip,
     )
 

time: 153 us -> 153 us (level)
    unnamed x20 -> x24, local copies, waits for them, and re-layouts: 4.46 us -> 5.33 us
where the time goes in v4:
time: 153 us; the launch traced here: 152 us
  waiting for transfers between devices  48.7 us (32%)
  starting transfers between devices  44.6 us (29%)
  Pallas kernels  36.3 us (24%)
  blocking collectives  16.1 us (11%)
  local copies, waits for them, and re-layouts  6.23 us (4%)
    all_to_all x3, waiting for transfers between devices, across(): return lax.all_to_all(x, PLANE, split_axis=0, concat_axis=0, tiled=True)  42.1 us
    all_to_all x3, starting transfers between devices, across(): return lax.all_to_all(x, PLANE, split_axis=0, concat_axis=0, tiled=True)  24 us
    all_to_all x1, blocking collectives, across(): return lax.all_to_all(x, PLANE, split_axis=0, concat_axis=0, tiled=True)  16.1 us
    pallas_call x2, Pallas kernels, convolve(): pl.pallas_call(functools.partial(conv_kernel, layout, len(sources), len(o...  14.5 us
    pallas_call x5, Pallas kernels, from_streams(): pl.pallas_call(kernel, in_specs=[pl.BlockSpec(memory_space=pltpu.SMEM), p...  12.2 us
    ppermute x5, starting transfers between devices, swap_planes(): return lax.ppermute(x, 'zh', [(0, 1), (1, 0)])  11.3 us
    ppermute x5, waiting for transfers between devices, swap_planes(): return lax.ppermute(x, 'zh', [(0, 1), (1, 0)])  6.6 us
    unnamed x24, local copies, waits for them, and re-layouts  5.33 us
  transfers between devices with their start and end apart: 12, of which 5 were waited for; matrix products, arithmetic and copies ran while one was open for 0% of the time, Pallas kernels for 22%

profile of v4, /device:TPU:1, one launch (start us, length us, event | category | flops | bytes accessed | tf_op | source)
XLA Modules:
  0.0 152.3 jit_solution(5872754288671441214)
XLA Ops:
  0.9 4.6 %collective-permute-start = (f32[3,8,1024]{2,1,0:T(8,128)S(1)}, f32[3,8,1024]{2,1,0:T(8,128)S(1)}, u32[]{:S(2)}, u32[]{:S(2)}) collective-permute-start(f32[3,8,1024]{2,1,0:T(8,128)S(1)} %slice.3), channel_id=1, source_target_pairs={{0,4},{4,8},{8,12},{12,16},{16,20},{20,24},{24,28},{28,32},{32,36}... | collective-permute-start | bytes 294920 | tf_op jit(solution)/shard_map/ppermute | solution.py:640
  5.5 3.1 %collective-permute-start.3 = (f32[4,128]{1,0:T(4,128)}, f32[4,128]{1,0:T(4,128)}, u32[]{:S(2)}, u32[]{:S(2)}) collective-permute-start(f32[4,128]{1,0:T(4,128)} %refs_0_.1), channel_id=1, source_target_pairs={{0,2},{1,3},{2,0},{3,1},{4,6},{5,7},{6,4},{7,5},{8,10},{9,11},{10,... | collective-permute-start | bytes 6152 | tf_op jit(solution)/shard_map/ppermute | solution.py:654
  8.6 1.6 %collective-permute-start.2 = (f32[4,128]{1,0:T(4,128)}, f32[4,128]{1,0:T(4,128)}, u32[]{:S(2)}, u32[]{:S(2)}) collective-permute-start(f32[4,128]{1,0:T(4,128)} %refs_0_.1), channel_id=1, source_target_pairs={{0,1},{1,0},{2,3},{3,2},{4,5},{5,4},{6,7},{7,6},{8,9},{9,8},{10,11... | collective-permute-start | bytes 6152 | tf_op jit(solution)/shard_map/ppermute | solution.py:654
  10.2 2.7 %streams.5 = (f32[32,4,8,128]{3,2,1,0:T(8,128)}, f32[512,256]{1,0:T(8,128)S(1)}) custom-call(s32[1]{0:T(128)} %bitcast.z_ref, f32[3,8,1024]{2,1,0:T(8,128)S(1)} %collective-permute-done.halo_ref, f32[3,7,1024]{2,1,0:T(8,128)} %short_ref.9, f32[3,512,1024]{2,1,0:T(8,128)} %proj_ref.9), custom_call_target="tpu_custom_call" | custom-call | flops 1000000 | bytes 1000000 | tf_op jit(solution)/shard_map/streams/pallas_call | solution.py:360
  12.9 5.9 %collective-permute-start.1 = (f32[32,4,8,128]{3,2,1,0:T(8,128)}, f32[32,4,8,128]{3,2,1,0:T(8,128)}, u32[]{:S(2)}, u32[]{:S(2)}) collective-permute-start(f32[32,4,8,128]{3,2,1,0:T(8,128)} %get-tuple-element.19), channel_id=1, source_target_pairs={{0,32},{32,0},{1,33},{33,1},{2,34},{34,2},{3,35},{35,3},{4,36},{36... | collective-permute-start | bytes 1572872 | tf_op jit(solution)/shard_map/ppermute | solution.py:531
  18.8 2.7 %streams.6 = (f32[32,4,8,128]{3,2,1,0:T(8,128)}, f32[512,256]{1,0:T(8,128)S(1)}) custom-call(s32[1]{0:T(128)} %bitcast.z_ref, f32[3,8,1024]{2,1,0:T(8,128)S(1)} %collective-permute-done.halo_ref, f32[3,7,1024]{2,1,0:T(8,128)} %short_ref.9, f32[3,512,1024]{2,1,0:T(8,128)} %proj_ref.9, f32[512,256]{1,0:T(8,128)S(1)} %get-tuple-element.16.rest_0_.a_product_ref), custom_call_target="tpu_custom_call" | custom-call | flops 1000000 | bytes 1000000 | tf_op jit(solution)/shard_map/streams/pallas_call | solution.py:360
  21.6 11.1 %all-to-all-start.1 = ((f32[32,4,8,128]{3,2,1,0:T(8,128)}), f32[32,4,8,128]{3,2,1,0:T(8,128)}, u32[]{:S(2)}, u32[]{:S(2)}) async-start(f32[32,4,8,128]{3,2,1,0:T(8,128)} %get-tuple-element.20), calls=%async_computation.1 | async-start | bytes 1048576 | tf_op jit(solution)/shard_map/all_to_all | solution.py:535
  32.6 2.9 %streams.7 = (f32[32,8,8,128]{3,2,1,0:T(8,128)S(1)}, f32[512,512]{1,0:T(8,128)S(1)}) custom-call(s32[1]{0:T(128)} %bitcast.z_ref, f32[3,8,1024]{2,1,0:T(8,128)S(1)} %collective-permute-done.halo_ref, f32[3,7,1024]{2,1,0:T(8,128)} %short_ref.9, f32[3,512,1024]{2,1,0:T(8,128)} %proj_ref.9, f32[512,256]{1,0:T(8,128)S(1)} %get-tuple-element.17.rest_0_.b_product_ref), custom_call_target="tpu_custom_call" | custom-call | flops 199999995904 | bytes 1000000 | tf_op jit(solution)/shard_map/streams/pallas_call | solution.py:360
  38.9 5.3 %all-to-all-done.1.rest_1_ = f32[32,4,8,128]{3,2,1,0:T(8,128)} async-done(((f32[32,4,8,128]{3,2,1,0:T(8,128)}), f32[32,4,8,128]{3,2,1,0:T(8,128)}, u32[]{:S(2)}, u32[]{:S(2)}) %all-to-all-start.1) | async-done | bytes 524320 | tf_op jit(solution)/shard_map/all_to_all | solution.py:535
  44.3 1.4 collective-permute-done.5.there_ref
  46.5 3.0 %rearrange.2 = f32[32,13,8,128]{3,2,1,0:T(8,128)} custom-call(s32[2]{0:T(128)S(1)} %pad_add_fusion.place_ref, f32[32,8,8,128]{3,2,1,0:T(8,128)} %copy-done.2, f32[32,4,8,128]{3,2,1,0:T(8,128)} %collective-permute-done.1.from_ref.rest_0_, f32[16,128]{1,0:T(8,128)S(1)} %copy-done.6, f32[16,128]{1,0:T(8,128)S(1)} %collective-permute-done.5.there_ref), custom_call_target="tpu_custom_call" | custom-call | flops 10000000000 | bytes 1000 | tf_op jit(solution)/shard_map/rearrange/pallas_call | solution.py:606
  49.5 8.4 %all-to-all-start = ((f32[32,13,8,128]{3,2,1,0:T(8,128)}), f32[32,13,8,128]{3,2,1,0:T(8,128)}, u32[]{:S(2)}, u32[]{:S(2)}) async-start(f32[32,13,8,128]{3,2,1,0:T(8,128)} %rearrange.2), calls=%async_computation | async-start | bytes 3407872 | tf_op jit(solution)/shard_map/all_to_all | solution.py:535
  57.9 1.9 %streams.8.refs_6_.gate_a_ref = f32[512,512]{1,0:T(8,128)S(1)} custom-call(s32[1]{0:T(128)} %bitcast.z_ref, f32[3,8,1024]{2,1,0:T(8,128)S(1)} %collective-permute-done.halo_ref, f32[3,7,1024]{2,1,0:T(8,128)} %short_ref.9, f32[3,512,1024]{2,1,0:T(8,128)} %proj_ref.9, f32[32,4,8,128]{3,2,1,0:T(8,128)} %collective-permute-done.1.from_ref.rest_0_, ...), custom_call_target="tpu_custom_call" | custom-call | flops 199999995904 | bytes 1000000 | tf_op jit(solution)/shard_map/streams/pallas_call | solution.py:360
  59.8 22.2 %all-to-all-done = f32[32,13,8,128]{3,2,1,0:T(8,128)} async-done(((f32[32,13,8,128]{3,2,1,0:T(8,128)}), f32[32,13,8,128]{3,2,1,0:T(8,128)}, u32[]{:S(2)}, u32[]{:S(2)}) %all-to-all-start) | async-done | bytes 1703968 | tf_op jit(solution)/shard_map/all_to_all | solution.py:535
  82.0 7.5 %convolve.2 = (f32[1024,128]{1,0:T(8,128)S(1)}, f32[1024,128]{1,0:T(8,128)S(1)}, f32[256,256]{1,0:T(8,128)S(1)}) custom-call(s32[1]{0:T(128)} %bitcast.z_ref, f32[3328,128]{1,0:T(8,128)} %bitcast.2.refs_0_, bf16[512,512]{1,0:T(8,128)(2,1)} %constant.20.clone.refs_1_.refs_3_, bf16[256,1024]{1,0:T(8,128)(2,1)} %constant.21.clone.refs_2_.refs_4_, ...), custom_call_target="tpu_custom_call" | custom-call | flops 10000000 | bytes 1000000 | tf_op jit(solution)/shard_map/convolve/pallas_call | solution.py:507
  90.6 7.0 %convolve.3 = (f32[1024,128]{1,0:T(8,128)S(1)}, f32[1024,128]{1,0:T(8,128)S(1)}) custom-call(s32[1]{0:T(128)} %bitcast.z_ref, f32[3328,128]{1,0:T(8,128)} %bitcast.2.refs_0_, f32[1024,128]{1,0:T(8,128)} %bitcast.5.refs_1_, f32[256,256]{1,0:T(8,128)S(1)} %get-tuple-element.23.refs_2_, bf16[512,512]{1,0:T(8,128)(2,1)} %constant.20.clone.refs_1_.refs_3_, ...), custom_call_target="tpu_custom_call" | custom-call | flops 10000000 | bytes 1000000 | tf_op jit(solution)/shard_map/convolve/pallas_call | solution.py:507
  97.7 16.1 %all_to_all.20.rest_1_ = f32[32,4,8,128]{3,2,1,0:T(8,128)} all-to-all(f32[32,4,8,128]{3,2,1,0:T(8,128)S(1)} %bitcast.9), channel_id=1, replica_groups=mesh['x'=4,'zh'=2,'y'=4,'core'=2,'zl'=4] {'x','y','core'}, dimensions={0} | all-to-all | bytes 1048576 | tf_op jit(solution)/shard_map/all_to_all | solution.py:535
  113.7 5.1 %collective-permute-start.8 = (f32[32,4,8,128]{3,2,1,0:T(8,128)}, f32[32,4,8,128]{3,2,1,0:T(8,128)}, u32[]{:S(2)}, u32[]{:S(2)}) collective-permute-start(f32[32,4,8,128]{3,2,1,0:T(8,128)} %all_to_all.20.rest_1_), channel_id=1, source_target_pairs={{0,32},{32,0},{1,33},{33,1},{2,34},{34,2},{3,35},{35,3},{4,36},{36... | collective-permute-start | bytes 1572872 | tf_op jit(solution)/shard_map/ppermute | solution.py:531
  118.9 2.2 %rearrange.3 = f32[32,12,8,128]{3,2,1,0:T(8,128)} custom-call(f32[32,4,8,128]{3,2,1,0:T(8,128)} %bitcast.11, f32[32,4,8,128]{3,2,1,0:T(8,128)S(1)} %collective-permute-done.6.from_ref.rest_0_, f32[32,4,8,128]{3,2,1,0:T(8,128)} %bitcast.13), custom_call_target="tpu_custom_call" | custom-call | flops 10000000000 | bytes 1000 | tf_op jit(solution)/shard_map/rearrange/pallas_call | solution.py:606
  121.9 4.5 %all-to-all-start.2 = ((f32[32,12,8,128]{3,2,1,0:T(8,128)}), f32[32,12,8,128]{3,2,1,0:T(8,128)}, u32[]{:S(2)}, u32[]{:S(2)}) async-start(f32[32,12,8,128]{3,2,1,0:T(8,128)} %rearrange.3), calls=%async_computation.2 | async-start | bytes 3145728 | tf_op jit(solution)/shard_map/all_to_all | solution.py:535
  127.5 2.0 %streams.9.gate_b_ref = f32[512,512]{1,0:T(8,128)S(1)} custom-call(s32[1]{0:T(128)} %bitcast.z_ref, f32[3,8,1024]{2,1,0:T(8,128)S(1)} %collective-permute-done.halo_ref, f32[3,7,1024]{2,1,0:T(8,128)} %short_ref.9, f32[3,512,1024]{2,1,0:T(8,128)} %proj_ref.9, f32[32,4,8,128]{3,2,1,0:T(8,128)S(1)} %copy-done.9, f32[32,4,8,128]{3,2,1,0:T(8,128)} %all_to_all.20.rest_1_), custom_call_target="tpu_custom_call" | custom-call | flops 199999995904 | bytes 1000000 | tf_op jit(solution)/shard_map/streams/pallas_call | solution.py:360
  129.4 5.1 %collective-permute-done.8.b_ref = f32[32,4,8,128]{3,2,1,0:T(8,128)} collective-permute-done((f32[32,4,8,128]{3,2,1,0:T(8,128)}, f32[32,4,8,128]{3,2,1,0:T(8,128)}, u32[]{:S(2)}, u32[]{:S(2)}) %collective-permute-start.8) | collective-permute-done | bytes 524320 | tf_op jit(solution)/shard_map/ppermute | solution.py:531
  134.6 14.5 %all-to-all-done.2.out_part_ref = f32[32,12,8,128]{3,2,1,0:T(8,128)} async-done(((f32[32,12,8,128]{3,2,1,0:T(8,128)}), f32[32,12,8,128]{3,2,1,0:T(8,128)}, u32[]{:S(2)}, u32[]{:S(2)}) %all-to-all-start.2) | async-done | bytes 1572896 | tf_op jit(solution)/shard_map/all_to_all | solution.py:535
  149.1 3.0 %finish.1 = f32[512,1024]{1,0:T(8,128)} custom-call(s32[1]{0:T(128)} %bitcast.z_ref, f32[32,12,8,128]{3,2,1,0:T(8,128)} %all-to-all-done.2.out_part_ref, f32[32,4,8,128]{3,2,1,0:T(8,128)} %collective-permute-done.8.b_ref, f32[512,512]{1,0:T(8,128)S(1)} %streams.8.refs_6_.gate_a_ref, f32[512,512]{1,0:T(8,128)S(1)} %streams.9.gate_b_ref, ...), custom_call_target="tpu_custom_call" | custom-call | flops 1000000 | bytes 1000000 | tf_op jit(solution)/shard_map/finish/pallas_call | solution.py:474
  (38 shorter events, 7.9 us)
Async XLA Ops:
  0.9 9.3 %collective-permute-start = (f32[3,8,1024]{2,1,0:T(8,128)S(1)}, f32[3,8,1024]{2,1,0:T(8,128)S(1)}, u32[]{:S(2)}, u32[]{:S(2)}) collective-permute-start(f32[3,8,1024]{2,1,0:T(8,128)S(1)} %slice.3), channel_id=1, source_target_pairs={{0,4},{4,8},{8,12},{12,16},{16,20},{20,24},{24,28},{28,32},{32,36}... | collective-permute-start | bytes 294920 | tf_op jit(solution)/shard_map/ppermute | solution.py:640
  5.5 32.1 %collective-permute-start.3 = (f32[4,128]{1,0:T(4,128)}, f32[4,128]{1,0:T(4,128)}, u32[]{:S(2)}, u32[]{:S(2)}) collective-permute-start(f32[4,128]{1,0:T(4,128)} %refs_0_.1), channel_id=1, source_target_pairs={{0,2},{1,3},{2,0},{3,1},{4,6},{5,7},{6,4},{7,5},{8,10},{9,11},{10,... | collective-permute-start | bytes 6152 | tf_op jit(solution)/shard_map/ppermute | solution.py:654
  8.6 29.0 %collective-permute-start.2 = (f32[4,128]{1,0:T(4,128)}, f32[4,128]{1,0:T(4,128)}, u32[]{:S(2)}, u32[]{:S(2)}) collective-permute-start(f32[4,128]{1,0:T(4,128)} %refs_0_.1), channel_id=1, source_target_pairs={{0,1},{1,0},{2,3},{3,2},{4,5},{5,4},{6,7},{7,6},{8,9},{9,8},{10,11... | collective-permute-start | bytes 6152 | tf_op jit(solution)/shard_map/ppermute | solution.py:654
  10.2 27.4 %collective-permute-start.4 = (f32[4,128]{1,0:T(4,128)}, f32[4,128]{1,0:T(4,128)}, u32[]{:S(2)}, u32[]{:S(2)}) collective-permute-start(f32[4,128]{1,0:T(4,128)} %refs_0_.1), channel_id=1, source_target_pairs={{0,3},{1,2},{2,1},{3,0},{4,7},{5,6},{6,5},{7,4},{8,11},{9,10},{10,... | collective-permute-start | bytes 6152 | tf_op jit(solution)/shard_map/ppermute | solution.py:654
  12.9 8.6 %copy-start = (f32[512,256]{1,0:T(8,128)}, f32[512,256]{1,0:T(8,128)S(1)}, u32[]{:S(2)}) copy-start(f32[512,256]{1,0:T(8,128)S(1)} %get-tuple-element.16.rest_0_.a_product_ref) | copy-start | bytes 1572868
  12.9 32.8 %collective-permute-start.1 = (f32[32,4,8,128]{3,2,1,0:T(8,128)}, f32[32,4,8,128]{3,2,1,0:T(8,128)}, u32[]{:S(2)}, u32[]{:S(2)}) collective-permute-start(f32[32,4,8,128]{3,2,1,0:T(8,128)} %get-tuple-element.19), channel_id=1, source_target_pairs={{0,32},{32,0},{1,33},{33,1},{2,34},{34,2},{3,35},{35,3},{4,36},{36... | collective-permute-start | bytes 1572872 | tf_op jit(solution)/shard_map/ppermute | solution.py:531
  21.5 14.0 %copy-start.4 = (f32[512,256]{1,0:T(8,128)}, f32[512,256]{1,0:T(8,128)S(1)}, u32[]{:S(2)}) copy-start(f32[512,256]{1,0:T(8,128)S(1)} %get-tuple-element.17.rest_0_.b_product_ref) | copy-start | bytes 1572868
  21.6 22.7 %all-to-all-start.1 = ((f32[32,4,8,128]{3,2,1,0:T(8,128)}), f32[32,4,8,128]{3,2,1,0:T(8,128)}, u32[]{:S(2)}, u32[]{:S(2)}) async-start(f32[32,4,8,128]{3,2,1,0:T(8,128)} %get-tuple-element.20), calls=%async_computation.1 | async-start | bytes 1048576 | tf_op jit(solution)/shard_map/all_to_all | solution.py:535
  35.6 1.0 copy-start.2
  36.6 1.0 copy-start.3
  38.9 6.9 %collective-permute-start.5 = (f32[16,128]{1,0:T(8,128)}, f32[16,128]{1,0:T(8,128)S(1)}, u32[]{:S(2)}, u32[]{:S(2)}) collective-permute-start(f32[16,128]{1,0:T(8,128)} %later.1.here_ref), channel_id=1, source_target_pairs={{0,32},{32,0},{1,33},{33,1},{2,34},{34,2},{3,35},{35,3},{4,36},{36... | collective-permute-start | bytes 24584 | tf_op jit(solution)/shard_map/ppermute | solution.py:531
  44.3 46.3 %collective-permute-start.7 = (f32[32,4,8,128]{3,2,1,0:T(8,128)}, f32[32,4,8,128]{3,2,1,0:T(8,128)}, u32[]{:S(2)}, u32[]{:S(2)}) collective-permute-start(f32[32,4,8,128]{3,2,1,0:T(8,128)} %all-to-all-done.1.rest_1_), channel_id=1, source_target_pairs={{0,32},{32,0},{1,33},{33,1},{2,34},{34,2},{3,35},{35,3},{4,36},{36... | collective-permute-start | bytes 1572872 | tf_op jit(solution)/shard_map/ppermute | solution.py:531
  45.8 0.7 copy-start.6
  49.5 32.5 %all-to-all-start = ((f32[32,13,8,128]{3,2,1,0:T(8,128)}), f32[32,13,8,128]{3,2,1,0:T(8,128)}, u32[]{:S(2)}, u32[]{:S(2)}) async-start(f32[32,13,8,128]{3,2,1,0:T(8,128)} %rearrange.2), calls=%async_computation | async-start | bytes 3407872 | tf_op jit(solution)/shard_map/all_to_all | solution.py:535
  89.5 0.8 copy-start.10
  90.4 28.5 %collective-permute-start.6 = (f32[32,4,8,128]{3,2,1,0:T(8,128)S(1)}, f32[32,4,8,128]{3,2,1,0:T(8,128)S(1)}, u32[]{:S(2)}, u32[]{:S(2)}) collective-permute-start(f32[32,4,8,128]{3,2,1,0:T(8,128)S(1)} %bitcast.12), channel_id=1, source_target_pairs={{0,32},{32,0},{1,33},{33,1},{2,34},{34,2},{3,35},{35,3},{4,36},{36... | collective-permute-start | bytes 1572872 | tf_op jit(solution)/shard_map/ppermute | solution.py:531
  97.6 21.2 %copy-start.11 = (f32[1024,128]{1,0:T(8,128)}, f32[1024,128]{1,0:T(8,128)S(1)}, u32[]{:S(2)}) copy-start(f32[1024,128]{1,0:T(8,128)S(1)} %get-tuple-element.24) | copy-start | bytes 1572868
  113.7 20.8 %collective-permute-start.8 = (f32[32,4,8,128]{3,2,1,0:T(8,128)}, f32[32,4,8,128]{3,2,1,0:T(8,128)}, u32[]{:S(2)}, u32[]{:S(2)}) collective-permute-start(f32[32,4,8,128]{3,2,1,0:T(8,128)} %all_to_all.20.rest_1_), channel_id=1, source_target_pairs={{0,32},{32,0},{1,33},{33,1},{2,34},{34,2},{3,35},{35,3},{4,36},{36... | collective-permute-start | bytes 1572872 | tf_op jit(solution)/shard_map/ppermute | solution.py:531
  121.1 0.8 copy-start.8
  121.9 27.2 %all-to-all-start.2 = ((f32[32,12,8,128]{3,2,1,0:T(8,128)}), f32[32,12,8,128]{3,2,1,0:T(8,128)}, u32[]{:S(2)}, u32[]{:S(2)}) async-start(f32[32,12,8,128]{3,2,1,0:T(8,128)} %rearrange.3), calls=%async_computation.2 | async-start | bytes 3145728 | tf_op jit(solution)/shard_map/all_to_all | solution.py:535
  126.4 1.0 copy-start.9
  127.5 21.7 %copy-start.1 = (f32[512,256]{1,0:T(8,128)S(1)}, f32[512,256]{1,0:T(8,128)}, u32[]{:S(2)}) copy-start(f32[512,256]{1,0:T(8,128)} %copy-done) | copy-start | bytes 1572868
  127.5 21.7 %copy-start.5 = (f32[512,256]{1,0:T(8,128)S(1)}, f32[512,256]{1,0:T(8,128)}, u32[]{:S(2)}) copy-start(f32[512,256]{1,0:T(8,128)} %copy-done.4) | copy-start | bytes 1572868
  127.5 21.7 %copy-start.7 = (f32[1024]{0:T(1024)S(1)}, f32[1024]{0:T(1024)}, u32[]{:S(2)}) copy-start(f32[1024]{0:T(1024)} %param.12) | copy-start | bytes 12292
